TPU v7x, 32 devices: a whole 2x2x4 slice. The times are simulated.
32 devices in a mesh: groups: 2 (over x), seq: 16 (over z, y, core), heads: 1.
Axes of the slice: x: 2, y: 2, z: 4, core: 2. Of those that a mesh axis runs over, the one named last changes fastest.
Arguments:
- x_rows: bfloat16 [10240, 3072], P(('groups', 'seq')), parts along dimension 0, may hold values from -0.125 to 0.125
- queries: bfloat16 [10240, 4096], P(('groups', 'seq'), 'heads'), parts along dimension 0, may hold values from -0.5 to 0.5
- keys: bfloat16 [10240, 4096], P(('groups', 'seq'), 'heads'), parts along dimension 0, may hold values from -0.5 to 0.5
- values: bfloat16 [10240, 4096], P(('groups', 'seq'), 'heads'), parts along dimension 0, may hold values from -0.75 to 0.75
- out_grad: bfloat16 [10240, 4096], P(('groups', 'seq'), 'heads'), parts along dimension 0, may hold values from -0.75 to 0.75
- log_decay: float32 [10240, 32], P(('groups', 'seq'), 'heads'), parts along dimension 0, may hold values from -4 to 0
Outputs:
- query_gradient: bfloat16 [10240, 4096], P(('groups', 'seq'), 'heads'), parts along dimension 0
- key_grad: bfloat16 [10240, 4096], P(('groups', 'seq'), 'heads'), parts along dimension 0
- value_grad: bfloat16 [10240, 4096], P(('groups', 'seq'), 'heads'), parts along dimension 0
- weight_grad: bfloat16 [6144, 4096], P(('groups', 'seq'), 'heads'), parts along dimension 0
There are 2 independent parts, one for each index of `groups`. A program takes and returns all parts, laid end to end along the dimension named above; each array names one. Nothing has to cross between parts.
All inputs are finite; a program needn't handle non-finite values.
Results may differ from a plain program's by a relative error of at most 0.033.
Values may be sent and summed in bfloat16 or wider, within the bound.
A program may use at most 192 MiB of HBM per device.

v0:
```python
import jax
import jax.numpy as jnp
from jax import lax
from jax.sharding import PartitionSpec as P


def block_states(queries, keys, values, output_gradients, cumul):
    span_total = cumul[-1]
    to_end = jnp.exp(span_total[None, :] - cumul)
    since_beginning = jnp.exp(cumul)
    weighted_key_rows = keys.astype(jnp.float32) * to_end[:, :, None]
    key_value_state = jnp.einsum(
        "yzf,yzu->zfu",
        weighted_key_rows,
        values.astype(jnp.float32),
        precision=lax.Precision.HIGHEST,
    )
    scaled_queries = queries.astype(jnp.float32) * since_beginning[:, :, None]
    qd_state = jnp.einsum(
        "thq,thv->hqv",
        scaled_queries,
        output_gradients.astype(jnp.float32),
        precision=lax.Precision.HIGHEST,
    )
    return (key_value_state.astype(jnp.bfloat16), qd_state.astype(jnp.bfloat16))


def block_grads(queries, keys, values, output_gradients, cumul, leading_product, suffix):
    length = queries.shape[0]
    span_total = cumul[-1]
    to_end = jnp.exp(span_total[None, :] - cumul)
    since_beginning = jnp.exp(cumul)
    heads_first = cumul.T
    gap_matrix = heads_first[:, :, None] - heads_first[:, None, :]
    steps_row = jnp.arange(length)
    causal = (steps_row[:, None] >= steps_row[None, :])[None]
    decays = jnp.where(causal, jnp.exp(jnp.where(causal, gap_matrix, 0.0)), 0.0)
    single_float = jnp.float32
    scores = jnp.einsum(
        "thv,shv->hts", output_gradients, values, preferred_element_type=single_float
    )
    weighted = (scores * decays).astype(jnp.bfloat16)
    pairs = jnp.einsum("thk,shk->hts", queries, keys, preferred_element_type=single_float)
    mixed = (pairs * decays).astype(jnp.bfloat16)
    query_gradient = jnp.einsum("hts,shk->thk", weighted, keys, preferred_element_type=single_float)
    query_gradient = query_gradient + since_beginning[:, :, None] * jnp.einsum(
        "znm,nxm->znx", output_gradients, leading_product, preferred_element_type=single_float
    )
    key_grad = jnp.einsum("hts,thk->shk", weighted, queries, preferred_element_type=single_float)
    key_grad = key_grad + to_end[:, :, None] * jnp.einsum(
        "shv,hqv->shq", values, suffix, preferred_element_type=single_float
    )
    value_grad = jnp.einsum(
        "hts,thv->shv", mixed, output_gradients, preferred_element_type=single_float
    )
    value_grad = value_grad + to_end[:, :, None] * jnp.einsum(
        "shq,hqv->shv", keys, suffix, preferred_element_type=single_float
    )
    return (
        query_gradient.astype(jnp.bfloat16),
        key_grad.astype(jnp.bfloat16),
        value_grad.astype(jnp.bfloat16),
    )


def on_device(x_rows, queries, keys, values, out_grad, log_decay):
    length, head_count = log_decay.shape
    head_size = queries.shape[1] // head_count
    shaped = (length, head_count, head_size)
    query_heads = queries.reshape(shaped)
    key_heads = keys.reshape(shaped)
    value_heads = values.reshape(shaped)
    grad_heads = out_grad.reshape(shaped)
    cumul = jnp.cumsum(log_decay, axis=0)
    span_total = cumul[-1]
    key_value_state, qd_state = block_states(query_heads, key_heads, value_heads, grad_heads, cumul)
    totals_all = lax.all_gather(span_total[None, :], "seq", axis=0, tiled=True)
    key_value_full, query_decay_full = (
        lax.all_gather(key_value_state[None], "seq", axis=0, tiled=True),
        lax.all_gather(qd_state[None], "seq", axis=0, tiled=True),
    )
    own_index = lax.axis_index("seq")
    before_sum = jnp.cumsum(totals_all, axis=0) - totals_all
    after_sum = before_sum + totals_all
    own_start = lax.dynamic_index_in_dim(before_sum, own_index, 0, keepdims=False)
    own_end = lax.dynamic_index_in_dim(after_sum, own_index, 0, keepdims=False)
    block_ids = jnp.arange(totals_all.shape[0])[:, None]
    earlier = block_ids < own_index
    later = block_ids > own_index
    preceding_weight = jnp.where(
        earlier, jnp.exp(jnp.where(earlier, own_start[None, :] - after_sum, 0.0)), 0.0
    )
    following_weight = jnp.where(
        later, jnp.exp(jnp.where(later, before_sum - own_end[None, :], 0.0)), 0.0
    )
    leading_product = jnp.einsum(
        "lc,lcyp->cyp",
        preceding_weight,
        key_value_full.astype(jnp.float32),
        precision=lax.Precision.HIGHEST,
    )
    suffix = jnp.einsum(
        "lc,lcyp->cyp",
        following_weight,
        query_decay_full.astype(jnp.float32),
        precision=lax.Precision.HIGHEST,
    )
    query_gradient, key_grad, value_grad = block_grads(
        query_heads,
        key_heads,
        value_heads,
        grad_heads,
        cumul,
        leading_product.astype(jnp.bfloat16),
        suffix.astype(jnp.bfloat16),
    )
    flat = (length, head_count * head_size)
    value_flat = value_grad.reshape(flat)
    weight_grad = lax.psum_scatter(
        jnp.einsum("td,tc->dc", x_rows, value_flat, preferred_element_type=jnp.float32).astype(
            jnp.bfloat16
        ),
        "seq",
        scatter_dimension=0,
        tiled=True,
    )
    return (query_gradient.reshape(flat), key_grad.reshape(flat), value_flat, weight_grad)


def solution(mesh):
    return jax.shard_map(
        on_device,
        mesh=mesh,
        in_specs=(
            P(("groups", "seq"), None),
            P(("groups", "seq"), "heads"),
            P(("groups", "seq"), "heads"),
            P(("groups", "seq"), "heads"),
            P(("groups", "seq"), "heads"),
            P(("groups", "seq"), "heads"),
        ),
        out_specs=(
            P(("groups", "seq"), "heads"),
            P(("groups", "seq"), "heads"),
            P(("groups", "seq"), "heads"),
            P(("groups", "seq"), "heads"),
        ),
        check_vma=False,
    )
```

profile of v0, /device:TPU:0, one launch (start us, length us, event | category | flops | bytes accessed | tf_op | source)
XLA Modules:
  0.0 530.0 jit_solution(6133120270504998837)
XLA Ops:
  7.2 1.0 copy_bitcast_fusion.3
  8.2 0.9 reduce-window.6
  9.6 9.1 %fusion.72 = bf16[32,128,128]{2,1,0:T(8,128)(2,1)} fusion(f32[320,32]{0,1:T(8,128)S(1)} %get-tuple-element.23, bf16[320,4096]{1,0:T(8,128)(2,1)} %param.7, bf16[320,4096]{1,0:T(8,128)(2,1)S(1)} %copy-done), kind=kOutput, calls=%fused_computation.66 | convolution fusion | flops 2016411648 | bytes 6332416 | tf_op jit(solution)/shard_map/thq,thv->hqv/dot_general | solution.py:19
  18.8 9.5 %fusion.67 = bf16[32,128,128]{2,1,0:T(8,128)(2,1)} fusion(f32[320,32]{0,1:T(8,128)S(1)} %get-tuple-element.22, bf16[320,4096]{1,0:T(8,128)(2,1)} %param.8, bf16[320,4096]{1,0:T(8,128)(2,1)} %param.9), kind=kOutput, calls=%fused_computation.65 | convolution fusion | flops 2016411648 | bytes 6332416 | tf_op jit(solution)/shard_map/yzf,yzu->zfu/dot_general | solution.py:12
  28.3 23.2 %all-gather.2 = f32[16,1,32]{2,1,0:T(1,128)S(1)} all-gather(f32[1,1,32]{2,1,0:T(1,128)S(1)} %bitcast.208), channel_id=1, replica_groups=mesh['groups'=2,'seq'=16,'heads'=1] {'seq'}, dimensions={0}, use_global_device_ids=true | all-gather | bytes 2176 | tf_op jit(solution)/shard_map/all_gather | solution.py:77
  51.9 10.7 %fusion.33 = f32[32,320,128]{2,1,0:T(8,128)} fusion(f32[32,320]{1,0:T(8,128)S(1)} %get-tuple-element.24, pred[320,320]{1,0:T(8,128)(4,1)S(1)} %iota_compare_fusion, bf16[320,4096]{1,0:T(8,128)(2,1)} %param.7, bf16[320,4096]{1,0:T(8,128)(2,1)} %param.8, bf16[320,4096]{1,0:T(8,128)(2,1)S(1)} %copy-done), kind=kOutput, calls=%fused_computation.43 | convolution fusion | flops 1694105600 | bytes 13250560 | tf_op jit(solution)/shard_map/hts,thv->shv/dot_general | solution.py:53
  62.6 85.9 %all-gather.8.cloned.1.call-done = bf16[512,128,128]{2,1,0:T(8,128)(2,1)} async-done(((bf16[32,128,128]{2,1,0:T(8,128)(2,1)}), bf16[512,128,128]{2,1,0:T(8,128)(2,1)}) %all-gather.8.cloned.1.call-update) | async-done | bytes 16777232 | tf_op jit(solution)/shard_map/all_gather | solution.py:80
  148.5 21.8 %fusion = f32[32,1,128,128]{3,1,2,0:T(1,128)S(1)} fusion(f32[16,32,1,1]{0,2,3,1:T(1,128)S(1)} %copy.96, bf16[16,32,128,128]{3,2,1,0:T(8,128)(2,1)} %bitcast.195), kind=kOutput, calls=%fused_computation.1 | convolution fusion | flops 100663296 | bytes 18876416 | tf_op jit(solution)/shard_map/lc,lcyp->cyp/dot_general | solution.py:102
  170.4 1.8 fusion.18
  172.2 2.2 copy.186
  174.4 20.1 %convert_bitcast_fusion = bf16[3072,4096]{0,1:T(8,128)(2,1)} fusion(bf16[320,4096]{1,0:T(8,128)(2,1)} %bitcast.199, bf16[320,3072]{1,0:T(8,128)(2,1)} %param.6), kind=kOutput, calls=%fused_computation | convolution fusion | flops 8065646592 | bytes 29753344 | tf_op jit(solution)/shard_map/td,tc->dc/dot_general | solution.py:120
  194.6 30.7 %copy.100 = bf16[3072,4096]{1,0:T(8,128)(2,1)} copy(bf16[3072,4096]{0,1:T(8,128)(2,1)} %convert_bitcast_fusion) | data formatting | bytes 50331648
  225.4 6.1 %multiply_convert_fusion.1 = bf16[32,320,320]{2,1,0:T(8,128)(2,1)S(1)} fusion(f32[32,320]{1,0:T(8,128)S(1)} %get-tuple-element.24, pred[320,320]{1,0:T(8,128)(4,1)S(1)} %iota_compare_fusion, bf16[320,4096]{1,0:T(8,128)(2,1)} %param.9, bf16[320,4096]{1,0:T(8,128)(2,1)S(1)} %copy-done), kind=kOutput, calls=%fused_computation.6 | convolution fusion | flops 855244800 | bytes 11939840 | tf_op jit(solution)/shard_map/thv,shv->hts/dot_general | solution.py:39
  231.5 6.7 %fusion.21 = f32[32,320,128]{2,1,0:T(8,128)} fusion(bf16[32,320,320]{2,1,0:T(8,128)(2,1)S(1)} %multiply_convert_fusion.1, bf16[320,4096]{1,0:T(8,128)(2,1)} %param.7), kind=kOutput, calls=%fused_computation.31 | convolution fusion | flops 838860800 | bytes 14417920 | tf_op jit(solution)/shard_map/hts,thk->shk/dot_general | solution.py:49
  238.2 4.2 fusion.27
  242.5 0.6 copy-done.3
  243.0 1.0 copy-done.7
  244.0 1.9 fusion.17
  245.9 2.2 copy.187
  248.1 28.2 %all-gather.6.cloned.1.call-done = bf16[512,128,128]{2,1,0:T(8,128)(2,1)} async-done(((bf16[32,128,128]{2,1,0:T(8,128)(2,1)}), bf16[512,128,128]{2,1,0:T(8,128)(2,1)}) %all-gather.6.cloned.1.call-update) | async-done | bytes 16777232 | tf_op jit(solution)/shard_map/all_gather | solution.py:79
  276.3 21.5 %fusion.2 = f32[32,1,128,128]{3,1,2,0:T(1,128)S(1)} fusion(f32[16,32,1,1]{0,2,3,1:T(1,128)S(1)} %copy.92, bf16[16,32,128,128]{3,2,1,0:T(8,128)(2,1)} %bitcast.194), kind=kOutput, calls=%fused_computation.3 | convolution fusion | flops 100663296 | bytes 18876416 | tf_op jit(solution)/shard_map/lc,lcyp->cyp/dot_general | solution.py:96
  297.8 5.1 fusion.16
  302.9 2.3 copy.188
  305.2 217.8 %reduce-scatter.4.cloned.1.call-done = bf16[192,4096]{1,0:T(8,128)(2,1)} async-done(((bf16[3072,4096]{1,0:T(8,128)(2,1)}), bf16[192,4096]{1,0:T(8,128)(2,1)}) %reduce-scatter.4.cloned.1.call-update) | async-done | bytes 1572880
  (35 shorter events, 1.2 us)
Async XLA Ops:
  7.2 2.5 copy-start
  7.2 141.3 %all-gather.8.cloned.1.call-start = ((), (), s32[]{:S(2)}) async-start(), calls=%async_computation.2 | async-start | bytes 17825792 | tf_op jit(solution)/shard_map/all_gather | solution.py:80
  18.7 257.6 %all-gather.6.cloned.1.call-start = ((), (), s32[]{:S(2)}) async-start(), calls=%async_computation.1 | async-start | bytes 17825792 | tf_op jit(solution)/shard_map/all_gather | solution.py:79
  28.3 494.8 %reduce-scatter.4.cloned.1.call-start = ((), (), s32[]{:S(2)}) async-start(), calls=%async_computation.3 | async-start | bytes 26738688
  148.5 21.9 %copy-start.4 = (bf16[320,4096]{1,0:T(8,128)(2,1)S(1)}, bf16[320,4096]{1,0:T(8,128)(2,1)}, u32[]{:S(2)}) copy-start(bf16[320,4096]{1,0:T(8,128)(2,1)} %param.8) | copy-start | bytes 7864324
  148.5 21.9 %copy-start.6 = (f32[32,320,128]{2,1,0:T(8,128)S(1)}, f32[32,320,128]{2,1,0:T(8,128)}, u32[]{:S(2)}) copy-start(f32[32,320,128]{2,1,0:T(8,128)} %fusion.33) | copy-start | bytes 15728644
  170.3 1.9 copy-start.1
  231.5 6.7 %copy-start.5 = (bf16[320,4096]{1,0:T(8,128)(2,1)S(1)}, bf16[320,4096]{1,0:T(8,128)(2,1)}, u32[]{:S(2)}) copy-start(bf16[320,4096]{1,0:T(8,128)(2,1)} %param.8) | copy-start | bytes 7864324
  238.2 4.2 copy-start.2
  238.2 4.8 copy-start.3
  238.2 5.8 %copy-start.7 = (bf16[320,4096]{1,0:T(8,128)(2,1)S(1)}, bf16[320,4096]{1,0:T(8,128)(2,1)}, u32[]{:S(2)}) copy-start(bf16[320,4096]{1,0:T(8,128)(2,1)} %param.9) | copy-start | bytes 7864324
Sparse Core Ops, SparseCore 0:
  18.8 129.5 all-gather.7
  151.2 125.0 all-gather.5
  281.0 242.0 reduce-scatter.3
where the time goes:
time: 539 us; the launch traced here: 530 us
  waiting for transfers between devices  332 us (62%)
  matrix products  119 us (22%)
  local copies, waits for them, and re-layouts  40.5 us (8%)
  blocking collectives  23.2 us (4%)
  between operations  14.4 us (3%)
    unnamed x4, waiting for transfers between devices  218 us
    all_gather x1, waiting for transfers between devices, on_device(): lax.all_gather(qd_state[None], 'seq', axis=0, tiled=True)  85.9 us
    unnamed x17, local copies, waits for them, and re-layouts  32.3 us
    all_gather x1, waiting for transfers between devices, on_device(): lax.all_gather(key_value_state[None], 'seq', axis=0, tiled=True)  28.2 us
    all_gather x1, blocking collectives, on_device(): totals_all = lax.all_gather(span_total[None, :], 'seq', axis=0, tiled=True)  23.2 us
    dot_general x1, matrix products, on_device(): jnp.einsum('lc,lcyp->cyp', following_weight, query_decay_full.astype(jnp....  21.8 us
    dot_general x1, matrix products, on_device(): jnp.einsum('lc,lcyp->cyp', preceding_weight, key_value_full.astype(jnp.fl...  21.5 us
    dot_general x1, matrix products, on_device(): jnp.einsum('td,tc->dc', x_rows, value_flat, preferred_element_type=jnp.fl...  20.1 us
  transfers between devices with their start and end apart: 3, of which 3 were waited for; matrix products, arithmetic and copies ran while one was open for 28% of the time, Pallas kernels for 0%

commit v1 on v0

v1 whole, which is shorter than its diff:
```python
import functools

import jax
import jax.numpy as jnp
from jax import lax
from jax.experimental import pallas as pl
from jax.experimental.pallas import tpu as pltpu
from jax.sharding import PartitionSpec as P

F32 = jnp.float32
BF16 = jnp.bfloat16
CHUNKS = 4


def dot(a, b, dims):
    return lax.dot_general(a, b, (dims, ((), ())), preferred_element_type=F32)


def columns_of(row, width):
    return jnp.broadcast_to(row, (width, row.shape[1])).T


def decay_matrix(row, width):
    length = row.shape[1]
    gap = columns_of(row, width)[:, :1] - row
    t = lax.broadcasted_iota(jnp.int32, (length, length), 0)
    s = lax.broadcasted_iota(jnp.int32, (length, length), 1)
    return jnp.where(t >= s, jnp.exp(jnp.where(t >= s, gap, 0.0)), 0.0)


def states_kernel(q_ref, k_ref, v_ref, g_ref, cum_ref, kv_ref, qd_ref):
    row = cum_ref[0]
    width = q_ref.shape[1]
    length = row.shape[1]
    cum = columns_of(row, width)
    total = row[:, length - 1 :]
    keys = (k_ref[...].astype(F32) * jnp.exp(total - cum)).astype(BF16)
    queries = (q_ref[...].astype(F32) * jnp.exp(cum)).astype(BF16)
    kv_ref[0] = dot(keys, v_ref[...], ((0,), (0,))).astype(BF16)
    qd_ref[0] = dot(queries, g_ref[...], ((0,), (0,))).astype(BF16)


def value_local_kernel(q_ref, k_ref, g_ref, cum_ref, out_ref):
    decays = decay_matrix(cum_ref[0], q_ref.shape[1])
    mixed = (dot(q_ref[...], k_ref[...], ((1,), (1,))) * decays).astype(BF16)
    out_ref[...] = dot(mixed, g_ref[...], ((0,), (0,)))


def value_finish_kernel(local_ref, k_ref, cum_ref, suffix_ref, out_ref):
    row = cum_ref[0]
    cum = columns_of(row, k_ref.shape[1])
    to_end = jnp.exp(row[:, row.shape[1] - 1 :] - cum)
    part = dot(k_ref[...], suffix_ref[0], ((1,), (0,)))
    out_ref[...] = (local_ref[...] + to_end * part).astype(BF16)


def query_key_kernel(q_ref, k_ref, v_ref, g_ref, cum_ref, prefix_ref, suffix_ref, qg_ref, kg_ref):
    row = cum_ref[0]
    width = q_ref.shape[1]
    cum = columns_of(row, width)
    to_end = jnp.exp(row[:, row.shape[1] - 1 :] - cum)
    decays = decay_matrix(row, width)
    weighted = (dot(g_ref[...], v_ref[...], ((1,), (1,))) * decays).astype(BF16)
    qg = dot(weighted, k_ref[...], ((1,), (0,)))
    qg = qg + jnp.exp(cum) * dot(g_ref[...], prefix_ref[0], ((1,), (1,)))
    kg = dot(weighted, q_ref[...], ((0,), (0,)))
    kg = kg + to_end * dot(v_ref[...], suffix_ref[0], ((1,), (1,)))
    qg_ref[...] = qg.astype(BF16)
    kg_ref[...] = kg.astype(BF16)


def per_head(body, first, count, length, size, kinds, outs, flops, args):
    specs = {
        "w": pl.BlockSpec((length, size), lambda h: (0, first + h)),
        "c": pl.BlockSpec((length, size), lambda h: (0, h)),
        "l": pl.BlockSpec((1, 1, length), lambda h: (first + h, 0, 0)),
        "s": pl.BlockSpec((1, size, size), lambda h: (h, 0, 0)),
    }
    shapes = {
        "c": (length, count * size),
        "s": (count, size, size),
    }
    moved = count * length * size * 2 * (len(kinds) + len(outs))
    return pl.pallas_call(
        body,
        grid=(count,),
        in_specs=[specs[kind] for kind in kinds],
        out_specs=[specs[kind] for kind, _ in outs],
        out_shape=[jax.ShapeDtypeStruct(shapes[kind], dtype) for kind, dtype in outs],
        cost_estimate=pl.CostEstimate(
            flops=count * flops, bytes_accessed=moved, transcendentals=count * length * length
        ),
        compiler_params=pltpu.CompilerParams(vmem_limit_bytes=32 * 1024 * 1024),
    )(*args)


def step(mapping, count):
    return [(i, mapping(i)) for i in range(count) if mapping(i) is not None]


def plane_scan(kv, qd, totals, index):
    heads = kv.shape[0]
    half = heads // 2
    z, y, c = index // 4, (index // 2) % 2, index % 2
    swap_core = step(lambda i: i ^ 1, 16)
    swap_chip = step(lambda i: i ^ 2, 16)
    onward = step(
        lambda i: (i + 4 if i + 4 < 16 else None) if i & 2 else (i - 4 if i >= 4 else None), 16
    )

    def mine(a, which):
        return lax.dynamic_slice_in_dim(a, which * half, half, axis=-3)

    stack = jnp.stack([kv, qd])
    got = lax.ppermute(mine(stack, 1 - c), "seq", swap_core)
    own = mine(stack, c)
    core0 = jnp.where(c == 0, own, got).astype(F32)
    core1 = jnp.where(c == 0, got, own).astype(F32)
    t = lax.dynamic_slice_in_dim(totals, c * half, half, axis=1).reshape(4, 2, 2, half)
    plane_totals = t.sum((1, 2))
    here = lax.dynamic_index_in_dim(t, z, 0, keepdims=False)
    own_chip = lax.dynamic_index_in_dim(here, y, 0, keepdims=False)
    other_chip = lax.dynamic_index_in_dim(here, 1 - y, 0, keepdims=False)

    def scale(log):
        return jnp.exp(log)[:, None, None]

    kv_chip = scale(own_chip[1]) * core0[0] + core1[0]
    qd_chip = core0[1] + scale(own_chip[0]) * core1[1]
    sent = jnp.where(y == 0, kv_chip, qd_chip).astype(BF16)
    neighbour = lax.ppermute(sent, "seq", swap_chip).astype(F32)
    plane = jnp.where(y == 0, qd_chip, kv_chip) + scale(own_chip.sum(0)) * neighbour
    travelling = plane.astype(BF16)
    direction = jnp.where(y == 0, 1, -1)
    beyond = jnp.zeros_like(plane)
    log = jnp.zeros((half,), F32)
    for hop in range(1, 4):
        travelling = lax.ppermute(travelling, "seq", onward)
        beyond = beyond + scale(log) * travelling.astype(F32)
        at = jnp.clip(z + direction * hop, 0, 3)
        log = log + lax.dynamic_index_in_dim(plane_totals, at, 0, keepdims=False)
    beyond = beyond.astype(BF16)
    other = lax.ppermute(beyond, "seq", swap_chip)
    before = jnp.where(y == 1, beyond, other).astype(F32)
    after = jnp.where(y == 0, beyond, other).astype(F32)
    other_scale = scale(other_chip.sum(0))
    before = jnp.where(y == 0, before, other_scale * before + neighbour)
    after = jnp.where(y == 1, after, other_scale * after + neighbour)
    for0 = jnp.stack([before, scale(own_chip[1]) * after + core1[1]])
    for1 = jnp.stack([scale(own_chip[0]) * before + core0[0], after])
    keep = jnp.where(c == 0, for0, for1).astype(BF16)
    give = jnp.where(c == 0, for1, for0).astype(BF16)
    took = lax.ppermute(give, "seq", swap_core)
    low = jnp.where(c == 0, keep, took)
    high = jnp.where(c == 0, took, keep)
    both = jnp.concatenate([low, high], axis=1)
    return both[0], both[1]


def gathered_scan(kv, qd, totals, index):
    kv_all = lax.all_gather(kv[None], "seq", axis=0, tiled=True)
    qd_all = lax.all_gather(qd[None], "seq", axis=0, tiled=True)
    before = jnp.cumsum(totals, axis=0) - totals
    after = before + totals
    own_start = lax.dynamic_index_in_dim(before, index, 0, keepdims=False)
    own_end = lax.dynamic_index_in_dim(after, index, 0, keepdims=False)
    ids = jnp.arange(totals.shape[0])[:, None]
    earlier, later = ids < index, ids > index
    pre = jnp.where(earlier, jnp.exp(jnp.where(earlier, own_start[None] - after, 0.0)), 0.0)
    post = jnp.where(later, jnp.exp(jnp.where(later, before - own_end[None], 0.0)), 0.0)
    prefix = jnp.sum(pre[:, :, None, None] * kv_all.astype(F32), axis=0)
    suffix = jnp.sum(post[:, :, None, None] * qd_all.astype(F32), axis=0)
    return prefix.astype(BF16), suffix.astype(BF16)


def plane_rows(x_rows, index):
    length, width = x_rows.shape
    place = index % 4
    parts = x_rows.reshape(length, 4, 4, width // 16)

    def columns(p):
        return lax.dynamic_index_in_dim(parts, p, 2, keepdims=False).reshape(length, width // 4)

    held = [columns(place)]
    for k in (1, 2, 3):
        held.append(lax.ppermute(columns(place ^ k), "seq", step(lambda i: i ^ k, 16)))
    return jnp.concatenate(held, axis=0).T


def plane_values(dv):
    core = lax.ppermute(dv, "seq", step(lambda i: i ^ 1, 16))
    chip = lax.ppermute(dv, "seq", step(lambda i: i ^ 2, 16))
    both = lax.ppermute(chip, "seq", step(lambda i: i ^ 1, 16))
    return jnp.concatenate([dv, core, chip, both], axis=0)


def planes_sum(blocks, index):
    z = index // 4

    def pick(i):
        return lax.dynamic_index_in_dim(blocks, jnp.clip(i, 0, 3), 0, keepdims=False)

    up = down = None
    for s in (1, 2, 3):
        to_up, to_down = pick(4 - s + z), pick(z - 4 + s)
        if up is not None:
            to_up = (to_up.astype(F32) + up.astype(F32)).astype(BF16)
            to_down = (to_down.astype(F32) + down.astype(F32)).astype(BF16)
        up = lax.ppermute(to_up, "seq", step(lambda i: i + 4 if i // 4 < s else None, 12))
        down = lax.ppermute(
            to_down, "seq", [(15 - a, 15 - b) for a, b in step(lambda i: i + 4 if i // 4 < s else None, 12)]
        )
    return (pick(z).astype(F32) + up.astype(F32) + down.astype(F32)).astype(BF16)


def on_device(blocks, x_rows, queries, keys, values, out_grad, log_decay):
    length, heads = log_decay.shape
    size = queries.shape[1] // heads
    index = lax.axis_index("seq")
    planes = blocks == 16 and x_rows.shape[1] % 16 == 0
    cumul = jnp.cumsum(log_decay, axis=0)
    lines = cumul.T[:, None, :]
    totals = lax.all_gather(cumul[-1:], "seq", axis=0, tiled=True)
    if planes:
        x_held = plane_rows(x_rows, index)
    chunks = CHUNKS if heads % (2 * CHUNKS) == 0 else 1
    count = heads // chunks
    square, state = 2 * length * length * size, 2 * length * size * size
    call = functools.partial(per_head, length=length, size=size)

    states = [
        call(
            states_kernel, i * count, count, kinds="wwwwl", outs=[("s", BF16)] * 2,
            flops=2 * state, args=(queries, keys, values, out_grad, lines),
        )
        for i in range(chunks)
    ]
    local = [
        call(
            value_local_kernel, i * count, count, kinds="wwwl", outs=[("c", F32)],
            flops=2 * square, args=(queries, keys, out_grad, lines),
        )[0]
        for i in range(chunks)
    ]
    scan = plane_scan if planes else gathered_scan
    prefixes, suffixes, value_grads, sums = [], [], [], []
    for i in range(chunks):
        own = slice(i * count, (i + 1) * count)
        prefix, suffix = scan(*states[i], totals[:, own], index)
        prefixes.append(prefix)
        suffixes.append(suffix)
        (dv,) = call(
            value_finish_kernel, i * count, count, kinds="cwls", outs=[("c", BF16)],
            flops=state, args=(local[i], keys, lines, suffix),
        )
        value_grads.append(dv)
        if planes:
            part = dot(x_held, plane_values(dv), ((1,), (0,))).astype(BF16)
            part = part.reshape(4, part.shape[0] // 4, part.shape[1])
            sums.append(planes_sum(part, index))
        else:
            part = dot(x_rows, dv, ((0,), (0,))).astype(BF16)
            sums.append(lax.psum_scatter(part, "seq", scatter_dimension=0, tiled=True))
    query_gradient, key_grad = call(
        query_key_kernel, 0, heads, kinds="wwwwlss", outs=[("c", BF16)] * 2,
        flops=3 * square + 2 * state,
        args=(
            queries, keys, values, out_grad, lines,
            jnp.concatenate(prefixes), jnp.concatenate(suffixes),
        ),
    )
    return (
        query_gradient,
        key_grad,
        jnp.concatenate(value_grads, axis=1),
        jnp.concatenate(sums, axis=1),
    )


def solution(mesh):
    spread = P(("groups", "seq"), "heads")
    return jax.shard_map(
        functools.partial(on_device, mesh.shape["seq"]),
        mesh=mesh,
        in_specs=(P(("groups", "seq"), None),) + (spread,) * 5,
        out_specs=(spread,) * 4,
        check_vma=False,
    )
```

time: 539 us -> 365 us (0.68)
  waiting for transfers between devices: 332 us -> 74.3 us
  matrix products: 119 us -> 8.77 us
  starting transfers between devices: 0.12 us -> 110 us
  Pallas kernels: 0 us -> 69.4 us
  other arithmetic: 1.31 us -> 23.8 us
  between operations: 14.4 us -> 2.43 us
  local copies, waits for them, and re-layouts: 40.5 us -> 49.1 us
    unnamed x4 -> x0, waiting for transfers between devices: 218 us -> none
    all_gather x2 -> x0, waiting for transfers between devices: 114 us -> none  [the longest x1 85.9 us: on_device(): lax.all_gather(qd_state[None], 'seq', axis=0, tiled=True)]
    dot_general x12 -> x4, matrix products: 119 us -> 8.77 us  [dot(): return lax.dot_general(a, b, (dims, ((), ())), preferred_element_type=F32)]
    ppermute x0 -> x67, starting transfers between devices: none -> 110 us  [the longest x12 60.4 us: planes_sum(): lax.ppermute(to_up, 'seq', step(lambda i: i + 4 if i // 4 < s else None,...]
    ppermute x0 -> x67, waiting for transfers between devices: none -> 74.3 us  [the longest x12 23.3 us: planes_sum(): lax.ppermute(to_up, 'seq', step(lambda i: i + 4 if i // 4 < s else None,...]
    pallas_call x0 -> x13, Pallas kernels: none -> 69.4 us  [per_head(): pl.pallas_call(body, grid=(count,), in_specs=[specs[kind] for kind in kin...]
    convert_element_type x0 -> x36, other arithmetic: none -> 13.4 us  [the longest x4 4.5 us: plane_scan(): beyond = beyond.astype(BF16)]
    ppermute x0 -> x3, local copies, waits for them, and re-layouts: none -> 6.26 us  [plane_rows(): lax.ppermute(columns(place ^ k), 'seq', step(lambda i: i ^ k, 16))]
  transfers between devices with their start and end apart: 3 -> 67, of which waited for: 3 -> 19; matrix products, arithmetic and copies ran while one was open for 28% -> 13% of each run, Pallas kernels for 0% -> 19%
where the time goes in v1:
time: 365 us; the launch traced here: 359 us
  starting transfers between devices  110 us (30%)
  waiting for transfers between devices  74.3 us (20%)
  Pallas kernels  69.4 us (19%)
  local copies, waits for them, and re-layouts  49.1 us (13%)
  other arithmetic  23.8 us (7%)
  blocking collectives  21.7 us (6%)
  matrix products  8.77 us (2%)
    pallas_call x13, Pallas kernels, per_head(): pl.pallas_call(body, grid=(count,), in_specs=[specs[kind] for kind in kin...  69.4 us
    ppermute x12, starting transfers between devices, planes_sum(): lax.ppermute(to_up, 'seq', step(lambda i: i + 4 if i // 4 < s else None,...  60.4 us
    unnamed x103, local copies, waits for them, and re-layouts  30.4 us
    ppermute x12, waiting for transfers between devices, planes_sum(): lax.ppermute(to_up, 'seq', step(lambda i: i + 4 if i // 4 < s else None,...  23.3 us
    ppermute x4, waiting for transfers between devices, plane_values(): chip = lax.ppermute(dv, 'seq', step(lambda i: i ^ 2, 16))  22 us
    all_gather x1, blocking collectives, on_device(): totals = lax.all_gather(cumul[-1:], 'seq', axis=0, tiled=True)  21.7 us
    ppermute x12, waiting for transfers between devices, planes_sum(): lax.ppermute(to_down, 'seq', [(15 - a, 15 - b) for a, b in step(lambda i:...  17.5 us
    ppermute x12, starting transfers between devices, plane_scan(): travelling = lax.ppermute(travelling, 'seq', onward)  15.8 us
  transfers between devices with their start and end apart: 67, of which 19 were waited for; matrix products, arithmetic and copies ran while one was open for 13% of the time, Pallas kernels for 19%

profile of v1, /device:TPU:0, one launch (start us, length us, event | category | flops | bytes accessed | tf_op | source)
XLA Modules:
  0.0 359.2 jit_solution(1170694642211869912)
XLA Ops:
  33.0 5.5 %shard_map.98.local_ref = f32[320,1024]{1,0:T(8,128)S(1)} custom-call(bf16[320,4096]{1,0:T(8,128)(2,1)S(1)} %copy-done.2, bf16[320,4096]{1,0:T(8,128)(2,1)S(1)} %copy-done, bf16[320,4096]{1,0:T(8,128)(2,1)S(1)} %copy-done.8, f32[32,1,320]{2,1,0:T(1,128)S(1)} %broadcast_in_dim.2.cum_ref), custom_call_target="tpu_custom_call" | custom-call | flops 419430400 | bytes 3276800 | tf_op jit(solution)/shard_map/pallas_call | solution.py:84
  39.6 21.7 %all-gather = f32[16,1,32]{2,1,0:T(1,128)S(1)} all-gather(f32[1,1,32]{2,1,0:T(1,128)S(1)} %bitcast.395), channel_id=1, replica_groups=mesh['groups'=2,'seq'=16,'heads'=1] {'seq'}, dimensions={0}, use_global_device_ids=true | all-gather | bytes 2176 | tf_op jit(solution)/shard_map/all_gather | solution.py:223
  82.9 5.6 %shard_map.100.local_ref = f32[320,1024]{1,0:T(8,128)S(1)} custom-call(bf16[320,4096]{1,0:T(8,128)(2,1)S(1)} %copy-done.4, bf16[320,4096]{1,0:T(8,128)(2,1)S(1)} %copy-done, bf16[320,4096]{1,0:T(8,128)(2,1)S(1)} %copy-done.10, f32[32,1,320]{2,1,0:T(1,128)S(1)} %broadcast_in_dim.2.cum_ref), custom_call_target="tpu_custom_call" | custom-call | flops 419430400 | bytes 3276800 | tf_op jit(solution)/shard_map/pallas_call | solution.py:84
  113.2 5.6 %shard_map.102.local_ref = f32[320,1024]{1,0:T(8,128)S(1)} custom-call(bf16[320,4096]{1,0:T(8,128)(2,1)S(1)} %copy-done.4, bf16[320,4096]{1,0:T(8,128)(2,1)S(1)} %copy-done, bf16[320,4096]{1,0:T(8,128)(2,1)S(1)} %copy-done.10, f32[32,1,320]{2,1,0:T(1,128)S(1)} %broadcast_in_dim.2.cum_ref), custom_call_target="tpu_custom_call" | custom-call | flops 419430400 | bytes 3276800 | tf_op jit(solution)/shard_map/pallas_call | solution.py:84
  128.6 5.6 %shard_map.104.local_ref = f32[320,1024]{1,0:T(8,128)S(1)} custom-call(bf16[320,4096]{1,0:T(8,128)(2,1)S(1)} %copy-done.5, bf16[320,4096]{1,0:T(8,128)(2,1)S(1)} %copy-done, bf16[320,4096]{1,0:T(8,128)(2,1)S(1)} %copy-done.11, f32[32,1,320]{2,1,0:T(1,128)S(1)} %broadcast_in_dim.2.cum_ref), custom_call_target="tpu_custom_call" | custom-call | flops 419430400 | bytes 3276800 | tf_op jit(solution)/shard_map/pallas_call | solution.py:84
  141.7 5.0 %concatenate.46 = bf16[1280,768]{0,1:T(8,128)(2,1)} concatenate(bf16[320,768]{0,1:T(8,128)(2,1)} %bitcast.383, bf16[320,768]{0,1:T(8,128)(2,1)} %copy.21, bf16[320,768]{0,1:T(8,128)(2,1)} %copy.22, bf16[320,768]{0,1:T(8,128)(2,1)} %copy.23), dimensions={0} | concatenate | bytes 3932160 | tf_op jit(solution)/shard_map/concatenate | solution.py:187
  152.1 7.6 %collective-permute-start.5 = (bf16[4,128,128]{2,1,0:T(8,128)(2,1)S(1)}, bf16[4,128,128]{2,1,0:T(8,128)(2,1)S(1)}, u32[]{:S(2)}, u32[]{:S(2)}) collective-permute-start(bf16[4,128,128]{2,1,0:T(8,128)(2,1)S(1)} %add_convert_fusion.3), channel_id=1, source_target_pairs={{0,2},{1,3},{2,0},{3,1},{4,6},{5,7},{6,4},{7,5},{8,10},{9,11},{10,... | collective-permute-start | bytes 393224 | tf_op jit(solution)/shard_map/ppermute | solution.py:143
  181.1 9.3 %collective-permute-done.32 = bf16[320,1024]{1,0:T(8,128)(2,1)S(1)} collective-permute-done((bf16[320,1024]{1,0:T(8,128)(2,1)S(1)}, bf16[320,1024]{1,0:T(8,128)(2,1)S(1)}, u32[]{:S(2)}, u32[]{:S(2)}) %collective-permute-start.32) | collective-permute-done | bytes 655392 | tf_op jit(solution)/shard_map/ppermute | solution.py:192
  190.4 24.4 %shard_map.97 = (bf16[320,4096]{1,0:T(8,128)(2,1)}, bf16[320,4096]{1,0:T(8,128)(2,1)}) custom-call(bf16[320,4096]{1,0:T(8,128)(2,1)S(1)} %copy-done.6, bf16[320,4096]{1,0:T(8,128)(2,1)S(1)} %copy-done, bf16[320,4096]{1,0:T(8,128)(2,1)S(1)} %copy-done.15, bf16[320,4096]{1,0:T(8,128)(2,1)S(1)} %copy-done.12, f32[32,1,320]{2,1,0:T(1,128)S(1)} %broadcast_in_dim.2.cum_ref, ...), custom_call_target="tpu_custom_call" | custom-call | flops 3187671040 | bytes 23592960 | tf_op jit(solution)/shard_map/pallas_call | solution.py:84
  222.8 12.8 %collective-permute-done.59 = bf16[320,1024]{1,0:T(8,128)(2,1)S(1)} collective-permute-done((bf16[320,1024]{1,0:T(8,128)(2,1)S(1)}, bf16[320,1024]{1,0:T(8,128)(2,1)S(1)}, u32[]{:S(2)}, u32[]{:S(2)}) %collective-permute-start.59) | collective-permute-done | bytes 655392 | tf_op jit(solution)/shard_map/ppermute | solution.py:192
  235.6 4.1 %collective-permute-start.34 = (bf16[192,1024]{1,0:T(8,128)(2,1)S(1)}, bf16[192,1024]{1,0:T(8,128)(2,1)S(1)}, u32[]{:S(2)}, u32[]{:S(2)}) collective-permute-start(bf16[192,1024]{1,0:T(8,128)(2,1)S(1)} %get-tuple-element.46), channel_id=1, source_target_pairs={{0,4},{1,5},{2,6},{3,7},{16,20},{17,21},{18,22},{19,23}} | collective-permute-start | bytes 1179656 | tf_op jit(solution)/shard_map/ppermute | solution.py:209
  251.7 5.9 %collective-permute-done.43 = bf16[192,1024]{1,0:T(8,128)(2,1)S(1)} collective-permute-done((bf16[192,1024]{1,0:T(8,128)(2,1)S(1)}, bf16[192,1024]{1,0:T(8,128)(2,1)S(1)}, u32[]{:S(2)}, u32[]{:S(2)}) %collective-permute-start.43) | collective-permute-done | bytes 393248 | tf_op jit(solution)/shard_map/ppermute | solution.py:209
  257.6 4.4 %collective-permute-start.61 = (bf16[192,1024]{1,0:T(8,128)(2,1)S(1)}, bf16[192,1024]{1,0:T(8,128)(2,1)S(1)}, u32[]{:S(2)}, u32[]{:S(2)}) collective-permute-start(bf16[192,1024]{1,0:T(8,128)(2,1)S(1)} %get-tuple-element.58), channel_id=1, source_target_pairs={{0,4},{1,5},{2,6},{3,7},{16,20},{17,21},{18,22},{19,23}} | collective-permute-start | bytes 1179656 | tf_op jit(solution)/shard_map/ppermute | solution.py:209
  262.1 3.9 %collective-permute-done.52 = bf16[192,1024]{1,0:T(8,128)(2,1)S(1)} collective-permute-done((bf16[192,1024]{1,0:T(8,128)(2,1)S(1)}, bf16[192,1024]{1,0:T(8,128)(2,1)S(1)}, u32[]{:S(2)}, u32[]{:S(2)}) %collective-permute-start.52) | collective-permute-done | bytes 393248 | tf_op jit(solution)/shard_map/ppermute | solution.py:209
  266.0 4.4 %collective-permute-start.35 = (bf16[192,1024]{1,0:T(8,128)(2,1)S(1)}, bf16[192,1024]{1,0:T(8,128)(2,1)S(1)}, u32[]{:S(2)}, u32[]{:S(2)}) collective-permute-start(bf16[192,1024]{1,0:T(8,128)(2,1)S(1)} %fusion.64), channel_id=1, source_target_pairs={{0,4},{1,5},{2,6},{3,7},{4,8},{5,9},{6,10},{7,11},{16,20},{17,21},... | collective-permute-start | bytes 1179656 | tf_op jit(solution)/shard_map/ppermute | solution.py:209
  270.5 3.9 %collective-permute-done.61 = bf16[192,1024]{1,0:T(8,128)(2,1)S(1)} collective-permute-done((bf16[192,1024]{1,0:T(8,128)(2,1)S(1)}, bf16[192,1024]{1,0:T(8,128)(2,1)S(1)}, u32[]{:S(2)}, u32[]{:S(2)}) %collective-permute-start.61) | collective-permute-done | bytes 393248 | tf_op jit(solution)/shard_map/ppermute | solution.py:209
  274.4 4.4 %collective-permute-start.44 = (bf16[192,1024]{1,0:T(8,128)(2,1)S(1)}, bf16[192,1024]{1,0:T(8,128)(2,1)S(1)}, u32[]{:S(2)}, u32[]{:S(2)}) collective-permute-start(bf16[192,1024]{1,0:T(8,128)(2,1)S(1)} %fusion.58), channel_id=1, source_target_pairs={{0,4},{1,5},{2,6},{3,7},{4,8},{5,9},{6,10},{7,11},{16,20},{17,21},... | collective-permute-start | bytes 1179656 | tf_op jit(solution)/shard_map/ppermute | solution.py:209
  282.8 4.4 %collective-permute-start.53 = (bf16[192,1024]{1,0:T(8,128)(2,1)S(1)}, bf16[192,1024]{1,0:T(8,128)(2,1)S(1)}, u32[]{:S(2)}, u32[]{:S(2)}) collective-permute-start(bf16[192,1024]{1,0:T(8,128)(2,1)S(1)} %fusion.52), channel_id=1, source_target_pairs={{0,4},{1,5},{2,6},{3,7},{4,8},{5,9},{6,10},{7,11},{16,20},{17,21},... | collective-permute-start | bytes 1179656 | tf_op jit(solution)/shard_map/ppermute | solution.py:209
  292.3 5.0 %collective-permute-start.36 = (bf16[192,1024]{1,0:T(8,128)(2,1)S(1)}, bf16[192,1024]{1,0:T(8,128)(2,1)S(1)}, u32[]{:S(2)}, u32[]{:S(2)}) collective-permute-start(bf16[192,1024]{1,0:T(8,128)(2,1)S(1)} %get-tuple-element.44), channel_id=1, source_target_pairs={{0,4},{1,5},{2,6},{3,7},{4,8},{5,9},{6,10},{7,11},{8,12},{9,13},{1... | collective-permute-start | bytes 1179656 | tf_op jit(solution)/shard_map/ppermute | solution.py:209
  300.7 5.0 %collective-permute-start.45 = (bf16[192,1024]{1,0:T(8,128)(2,1)S(1)}, bf16[192,1024]{1,0:T(8,128)(2,1)S(1)}, u32[]{:S(2)}, u32[]{:S(2)}) collective-permute-start(bf16[192,1024]{1,0:T(8,128)(2,1)S(1)} %get-tuple-element.48), channel_id=1, source_target_pairs={{0,4},{1,5},{2,6},{3,7},{4,8},{5,9},{6,10},{7,11},{8,12},{9,13},{1... | collective-permute-start | bytes 1179656 | tf_op jit(solution)/shard_map/ppermute | solution.py:209
  309.1 5.0 %collective-permute-start.54 = (bf16[192,1024]{1,0:T(8,128)(2,1)S(1)}, bf16[192,1024]{1,0:T(8,128)(2,1)S(1)}, u32[]{:S(2)}, u32[]{:S(2)}) collective-permute-start(bf16[192,1024]{1,0:T(8,128)(2,1)S(1)} %get-tuple-element.52), channel_id=1, source_target_pairs={{0,4},{1,5},{2,6},{3,7},{4,8},{5,9},{6,10},{7,11},{8,12},{9,13},{1... | collective-permute-start | bytes 1179656 | tf_op jit(solution)/shard_map/ppermute | solution.py:209
  318.1 18.9 %collective-permute-start.63 = (bf16[192,1024]{1,0:T(8,128)(2,1)S(1)}, bf16[192,1024]{1,0:T(8,128)(2,1)S(1)}, u32[]{:S(2)}, u32[]{:S(2)}) collective-permute-start(bf16[192,1024]{1,0:T(8,128)(2,1)S(1)} %get-tuple-element.56), channel_id=1, source_target_pairs={{0,4},{1,5},{2,6},{3,7},{4,8},{5,9},{6,10},{7,11},{8,12},{9,13},{1... | collective-permute-start | bytes 1179656 | tf_op jit(solution)/shard_map/ppermute | solution.py:209
  341.1 12.2 %collective-permute-done.57 = bf16[192,1024]{1,0:T(8,128)(2,1)S(1)} collective-permute-done((bf16[192,1024]{1,0:T(8,128)(2,1)S(1)}, bf16[192,1024]{1,0:T(8,128)(2,1)S(1)}, u32[]{:S(2)}, u32[]{:S(2)}) %collective-permute-start.57) | collective-permute-done | bytes 393248 | tf_op jit(solution)/shard_map/ppermute | solution.py:210
  353.5 4.2 %collective-permute-done.66 = bf16[192,1024]{1,0:T(8,128)(2,1)S(1)} collective-permute-done((bf16[192,1024]{1,0:T(8,128)(2,1)S(1)}, bf16[192,1024]{1,0:T(8,128)(2,1)S(1)}, u32[]{:S(2)}, u32[]{:S(2)}) %collective-permute-start.66) | collective-permute-done | bytes 393248 | tf_op jit(solution)/shard_map/ppermute | solution.py:210
  (338 shorter events, 168.1 us)
Async XLA Ops:
  7.1 101.0 %collective-permute-start.28 = (bf16[320,768]{1,0:T(8,128)(2,1)}, bf16[320,768]{1,0:T(8,128)(2,1)}, u32[]{:S(2)}, u32[]{:S(2)}) collective-permute-start(bf16[320,768]{1,0:T(8,128)(2,1)} %copy.18), channel_id=1, source_target_pairs={{0,1},{1,0},{2,3},{3,2},{4,5},{5,4},{6,7},{7,6},{8,9},{9,8},{10,11... | collective-permute-start | bytes 1474568 | tf_op jit(solution)/shard_map/ppermute | solution.py:186
  9.6 99.8 %collective-permute-start.29 = (bf16[320,768]{1,0:T(8,128)(2,1)}, bf16[320,768]{1,0:T(8,128)(2,1)}, u32[]{:S(2)}, u32[]{:S(2)}) collective-permute-start(bf16[320,768]{1,0:T(8,128)(2,1)} %copy.19), channel_id=1, source_target_pairs={{0,2},{1,3},{2,0},{3,1},{4,6},{5,7},{6,4},{7,5},{8,10},{9,11},{10,... | collective-permute-start | bytes 1474568 | tf_op jit(solution)/shard_map/ppermute | solution.py:186
  13.2 126.4 %collective-permute-start.30 = (bf16[320,768]{1,0:T(8,128)(2,1)}, bf16[320,768]{1,0:T(8,128)(2,1)}, u32[]{:S(2)}, u32[]{:S(2)}) collective-permute-start(bf16[320,768]{1,0:T(8,128)(2,1)} %copy.20), channel_id=1, source_target_pairs={{0,3},{1,2},{2,1},{3,0},{4,7},{5,6},{6,5},{7,4},{8,11},{9,10},{10,... | collective-permute-start | bytes 1474568 | tf_op jit(solution)/shard_map/ppermute | solution.py:186
  24.3 64.2 %collective-permute-start = (bf16[2,4,128,128]{3,2,1,0:T(8,128)(2,1)}, bf16[2,4,128,128]{3,2,1,0:T(8,128)(2,1)}, u32[]{:S(2)}, u32[]{:S(2)}) collective-permute-start(bf16[2,4,128,128]{3,2,1,0:T(8,128)(2,1)} %fusion.90), channel_id=1, source_target_pairs={{0,1},{1,0},{2,3},{3,2},{4,5},{5,4},{6,7},{7,6},{8,9},{9,8},{10,11... | collective-permute-start | bytes 786440 | tf_op jit(solution)/shard_map/ppermute | solution.py:115
  28.9 61.4 %collective-permute-start.7 = (bf16[2,4,128,128]{3,2,1,0:T(8,128)(2,1)}, bf16[2,4,128,128]{3,2,1,0:T(8,128)(2,1)}, u32[]{:S(2)}, u32[]{:S(2)}) collective-permute-start(bf16[2,4,128,128]{3,2,1,0:T(8,128)(2,1)} %fusion.88), channel_id=1, source_target_pairs={{0,1},{1,0},{2,3},{3,2},{4,5},{5,4},{6,7},{7,6},{8,9},{9,8},{10,11... | collective-permute-start | bytes 786440 | tf_op jit(solution)/shard_map/ppermute | solution.py:115
  119.9 26.7 %collective-permute-start.10 = (bf16[4,128,128]{2,1,0:T(8,128)(2,1)}, bf16[4,128,128]{2,1,0:T(8,128)(2,1)}, u32[]{:S(2)}, u32[]{:S(2)}) collective-permute-start(bf16[4,128,128]{2,1,0:T(8,128)(2,1)} %collective-permute-done.9), channel_id=1, source_target_pairs={{2,6},{3,7},{4,0},{5,1},{6,10},{7,11},{8,4},{9,5},{10,14},{11,15},... | collective-permute-start | bytes 393224 | tf_op jit(solution)/shard_map/ppermute | solution.py:138
  121.2 26.9 %collective-permute-start.17 = (bf16[4,128,128]{2,1,0:T(8,128)(2,1)}, bf16[4,128,128]{2,1,0:T(8,128)(2,1)}, u32[]{:S(2)}, u32[]{:S(2)}) collective-permute-start(bf16[4,128,128]{2,1,0:T(8,128)(2,1)} %collective-permute-done.16), channel_id=1, source_target_pairs={{2,6},{3,7},{4,0},{5,1},{6,10},{7,11},{8,4},{9,5},{10,14},{11,15},... | collective-permute-start | bytes 393224 | tf_op jit(solution)/shard_map/ppermute | solution.py:138
  122.6 26.9 %collective-permute-start.24 = (bf16[4,128,128]{2,1,0:T(8,128)(2,1)}, bf16[4,128,128]{2,1,0:T(8,128)(2,1)}, u32[]{:S(2)}, u32[]{:S(2)}) collective-permute-start(bf16[4,128,128]{2,1,0:T(8,128)(2,1)} %collective-permute-done.23), channel_id=1, source_target_pairs={{2,6},{3,7},{4,0},{5,1},{6,10},{7,11},{8,4},{9,5},{10,14},{11,15},... | collective-permute-start | bytes 393224 | tf_op jit(solution)/shard_map/ppermute | solution.py:138
  123.9 27.0 %collective-permute-start.4 = (bf16[4,128,128]{2,1,0:T(8,128)(2,1)}, bf16[4,128,128]{2,1,0:T(8,128)(2,1)}, u32[]{:S(2)}, u32[]{:S(2)}) collective-permute-start(bf16[4,128,128]{2,1,0:T(8,128)(2,1)} %collective-permute-done.3), channel_id=1, source_target_pairs={{2,6},{3,7},{4,0},{5,1},{6,10},{7,11},{8,4},{9,5},{10,14},{11,15},... | collective-permute-start | bytes 393224 | tf_op jit(solution)/shard_map/ppermute | solution.py:138
  173.8 44.5 %collective-permute-start.31 = (bf16[320,1024]{1,0:T(8,128)(2,1)S(1)}, bf16[320,1024]{1,0:T(8,128)(2,1)S(1)}, u32[]{:S(2)}, u32[]{:S(2)}) collective-permute-start(bf16[320,1024]{1,0:T(8,128)(2,1)S(1)} %shard_map.99), channel_id=1, source_target_pairs={{0,1},{1,0},{2,3},{3,2},{4,5},{5,4},{6,7},{7,6},{8,9},{9,8},{10,11... | collective-permute-start | bytes 1966088 | tf_op jit(solution)/shard_map/ppermute | solution.py:191
  176.2 42.6 %collective-permute-start.41 = (bf16[320,1024]{1,0:T(8,128)(2,1)S(1)}, bf16[320,1024]{1,0:T(8,128)(2,1)S(1)}, u32[]{:S(2)}, u32[]{:S(2)}) collective-permute-start(bf16[320,1024]{1,0:T(8,128)(2,1)S(1)} %shard_map.101), channel_id=1, source_target_pairs={{0,2},{1,3},{2,0},{3,1},{4,6},{5,7},{6,4},{7,5},{8,10},{9,11},{10,... | collective-permute-start | bytes 1966088 | tf_op jit(solution)/shard_map/ppermute | solution.py:192
  177.3 44.8 %collective-permute-start.40 = (bf16[320,1024]{1,0:T(8,128)(2,1)S(1)}, bf16[320,1024]{1,0:T(8,128)(2,1)S(1)}, u32[]{:S(2)}, u32[]{:S(2)}) collective-permute-start(bf16[320,1024]{1,0:T(8,128)(2,1)S(1)} %shard_map.101), channel_id=1, source_target_pairs={{0,1},{1,0},{2,3},{3,2},{4,5},{5,4},{6,7},{7,6},{8,9},{9,8},{10,11... | collective-permute-start | bytes 1966088 | tf_op jit(solution)/shard_map/ppermute | solution.py:191
  179.5 43.2 %collective-permute-start.50 = (bf16[320,1024]{1,0:T(8,128)(2,1)S(1)}, bf16[320,1024]{1,0:T(8,128)(2,1)S(1)}, u32[]{:S(2)}, u32[]{:S(2)}) collective-permute-start(bf16[320,1024]{1,0:T(8,128)(2,1)S(1)} %shard_map.103), channel_id=1, source_target_pairs={{0,2},{1,3},{2,0},{3,1},{4,6},{5,7},{6,4},{7,5},{8,10},{9,11},{10,... | collective-permute-start | bytes 1966088 | tf_op jit(solution)/shard_map/ppermute | solution.py:192
  190.4 29.5 %collective-permute-start.33 = (bf16[320,1024]{1,0:T(8,128)(2,1)S(1)}, bf16[320,1024]{1,0:T(8,128)(2,1)S(1)}, u32[]{:S(2)}, u32[]{:S(2)}) collective-permute-start(bf16[320,1024]{1,0:T(8,128)(2,1)S(1)} %collective-permute-done.32), channel_id=1, source_target_pairs={{0,1},{1,0},{2,3},{3,2},{4,5},{5,4},{6,7},{7,6},{8,9},{9,8},{10,11... | collective-permute-start | bytes 1966088 | tf_op jit(solution)/shard_map/ppermute | solution.py:193
  218.4 23.6 %collective-permute-start.49 = (bf16[320,1024]{1,0:T(8,128)(2,1)S(1)}, bf16[320,1024]{1,0:T(8,128)(2,1)S(1)}, u32[]{:S(2)}, u32[]{:S(2)}) collective-permute-start(bf16[320,1024]{1,0:T(8,128)(2,1)S(1)} %shard_map.103), channel_id=1, source_target_pairs={{0,1},{1,0},{2,3},{3,2},{4,5},{5,4},{6,7},{7,6},{8,9},{9,8},{10,11... | collective-permute-start | bytes 1966088 | tf_op jit(solution)/shard_map/ppermute | solution.py:191
  222.2 24.2 %collective-permute-start.58 = (bf16[320,1024]{1,0:T(8,128)(2,1)S(1)}, bf16[320,1024]{1,0:T(8,128)(2,1)S(1)}, u32[]{:S(2)}, u32[]{:S(2)}) collective-permute-start(bf16[320,1024]{1,0:T(8,128)(2,1)S(1)} %shard_map.105), channel_id=1, source_target_pairs={{0,1},{1,0},{2,3},{3,2},{4,5},{5,4},{6,7},{7,6},{8,9},{9,8},{10,11... | collective-permute-start | bytes 1966088 | tf_op jit(solution)/shard_map/ppermute | solution.py:191
  242.0 36.9 %collective-permute-start.37 = (bf16[192,1024]{1,0:T(8,128)(2,1)S(1)}, bf16[192,1024]{1,0:T(8,128)(2,1)S(1)}, u32[]{:S(2)}, u32[]{:S(2)}) collective-permute-start(bf16[192,1024]{1,0:T(8,128)(2,1)S(1)} %get-tuple-element.47), channel_id=1, source_target_pairs={{15,11},{14,10},{13,9},{12,8},{31,27},{30,26},{29,25},{28,24}} | collective-permute-start | bytes 1179656 | tf_op jit(solution)/shard_map/ppermute | solution.py:210
  246.3 41.2 %collective-permute-start.46 = (bf16[192,1024]{1,0:T(8,128)(2,1)S(1)}, bf16[192,1024]{1,0:T(8,128)(2,1)S(1)}, u32[]{:S(2)}, u32[]{:S(2)}) collective-permute-start(bf16[192,1024]{1,0:T(8,128)(2,1)S(1)} %get-tuple-element.51), channel_id=1, source_target_pairs={{15,11},{14,10},{13,9},{12,8},{31,27},{30,26},{29,25},{28,24}} | collective-permute-start | bytes 1179656 | tf_op jit(solution)/shard_map/ppermute | solution.py:210
  250.9 41.4 %collective-permute-start.55 = (bf16[192,1024]{1,0:T(8,128)(2,1)S(1)}, bf16[192,1024]{1,0:T(8,128)(2,1)S(1)}, u32[]{:S(2)}, u32[]{:S(2)}) collective-permute-start(bf16[192,1024]{1,0:T(8,128)(2,1)S(1)} %get-tuple-element.55), channel_id=1, source_target_pairs={{15,11},{14,10},{13,9},{12,8},{31,27},{30,26},{29,25},{28,24}} | collective-permute-start | bytes 1179656 | tf_op jit(solution)/shard_map/ppermute | solution.py:210
  292.3 25.8 %collective-permute-start.36 = (bf16[192,1024]{1,0:T(8,128)(2,1)S(1)}, bf16[192,1024]{1,0:T(8,128)(2,1)S(1)}, u32[]{:S(2)}, u32[]{:S(2)}) collective-permute-start(bf16[192,1024]{1,0:T(8,128)(2,1)S(1)} %get-tuple-element.44), channel_id=1, source_target_pairs={{0,4},{1,5},{2,6},{3,7},{4,8},{5,9},{6,10},{7,11},{8,12},{9,13},{1... | collective-permute-start | bytes 1179656 | tf_op jit(solution)/shard_map/ppermute | solution.py:209
  300.7 37.8 %collective-permute-start.45 = (bf16[192,1024]{1,0:T(8,128)(2,1)S(1)}, bf16[192,1024]{1,0:T(8,128)(2,1)S(1)}, u32[]{:S(2)}, u32[]{:S(2)}) collective-permute-start(bf16[192,1024]{1,0:T(8,128)(2,1)S(1)} %get-tuple-element.48), channel_id=1, source_target_pairs={{0,4},{1,5},{2,6},{3,7},{4,8},{5,9},{6,10},{7,11},{8,12},{9,13},{1... | collective-permute-start | bytes 1179656 | tf_op jit(solution)/shard_map/ppermute | solution.py:209
  309.1 31.9 %collective-permute-start.54 = (bf16[192,1024]{1,0:T(8,128)(2,1)S(1)}, bf16[192,1024]{1,0:T(8,128)(2,1)S(1)}, u32[]{:S(2)}, u32[]{:S(2)}) collective-permute-start(bf16[192,1024]{1,0:T(8,128)(2,1)S(1)} %get-tuple-element.52), channel_id=1, source_target_pairs={{0,4},{1,5},{2,6},{3,7},{4,8},{5,9},{6,10},{7,11},{8,12},{9,13},{1... | collective-permute-start | bytes 1179656 | tf_op jit(solution)/shard_map/ppermute | solution.py:209
  316.6 24.2 %collective-permute-start.48 = (bf16[192,1024]{1,0:T(8,128)(2,1)S(1)}, bf16[192,1024]{1,0:T(8,128)(2,1)S(1)}, u32[]{:S(2)}, u32[]{:S(2)}) collective-permute-start(bf16[192,1024]{1,0:T(8,128)(2,1)S(1)} %fusion.57), channel_id=1, source_target_pairs={{15,11},{14,10},{13,9},{12,8},{11,7},{10,6},{9,5},{8,4},{7,3},{6,2... | collective-permute-start | bytes 1179656 | tf_op jit(solution)/shard_map/ppermute | solution.py:210
  318.1 35.5 %collective-permute-start.63 = (bf16[192,1024]{1,0:T(8,128)(2,1)S(1)}, bf16[192,1024]{1,0:T(8,128)(2,1)S(1)}, u32[]{:S(2)}, u32[]{:S(2)}) collective-permute-start(bf16[192,1024]{1,0:T(8,128)(2,1)S(1)} %get-tuple-element.56), channel_id=1, source_target_pairs={{0,4},{1,5},{2,6},{3,7},{4,8},{5,9},{6,10},{7,11},{8,12},{9,13},{1... | collective-permute-start | bytes 1179656 | tf_op jit(solution)/shard_map/ppermute | solution.py:209
  (94 other events, 837.0 us)

commit v2 on v1

--- a/solution.py
+++ b/solution.py
@@ -92,6 +92,212 @@
         ),
         compiler_params=pltpu.CompilerParams(vmem_limit_bytes=32 * 1024 * 1024),
     )(*args)
+
+
+def mega_kernel(
+    blocks, x_ref, q_ref, k_ref, v_ref, g_ref, cum_ref, prefix_ref, suffix_ref,
+    qg_ref, kg_ref, dv_ref, wg_ref,
+    held, part, landed, plane_send, plane_recv, line_send, line_recv,
+):
+    index = lax.axis_index("seq")
+    z = index // 4
+    last = blocks // 4 - 1
+    core, chip = index + 1 - 2 * (index % 2), index + 2 - 4 * ((index // 2) % 2)
+    chunks, length, width = held.shape[0], q_ref.shape[0], held.shape[2]
+    size = prefix_ref.shape[1]
+    group = width // size
+    rows = part.shape[2]
+
+    barrier = pltpu.get_barrier_semaphore()
+
+    def greet(device):
+        pl.semaphore_signal(
+            barrier, inc=1, device_id={"seq": device}, device_id_type=pl.DeviceIdType.MESH
+        )
+
+    greet(core)
+    greet(chip)
+
+    @pl.when(z > 0)
+    def _():
+        greet(index - 4)
+
+    @pl.when(z < last)
+    def _():
+        greet(index + 4)
+
+    inner = (z > 0) & (z < last)
+    pl.when(inner)(lambda: pl.semaphore_wait(barrier, 4))
+    pl.when(jnp.logical_not(inner))(lambda: pl.semaphore_wait(barrier, 3))
+
+    def plane_copy(j, source, target, device):
+        return pltpu.make_async_remote_copy(
+            src_ref=held.at[j, pl.ds(source * length, length)],
+            dst_ref=held.at[j, pl.ds(target * length, length)],
+            send_sem=plane_send.at[target - 1, j],
+            recv_sem=plane_recv.at[target - 1, j],
+            device_id={"seq": device},
+            device_id_type=pl.DeviceIdType.MESH,
+        )
+
+    def to_core(j):
+        return plane_copy(j, 0, 1, core)
+
+    def to_chip(j):
+        return plane_copy(j, 0, 2, chip)
+
+    def onward(j):
+        return plane_copy(j, 2, 3, core)
+
+    def line_copy(j, way, t):
+        slot = t - 1 + way
+        return pltpu.make_async_remote_copy(
+            src_ref=part.at[j, t],
+            dst_ref=landed.at[way, slot, j],
+            send_sem=line_send.at[way, slot, j],
+            recv_sem=line_recv.at[way, slot, j],
+            device_id={"seq": index + 4 - 8 * way},
+            device_id_type=pl.DeviceIdType.MESH,
+        )
+
+    def columns(j, h):
+        return pl.ds(pl.multiple_of(j * width + h * size, size), size)
+
+    def value_part(j):
+        for h in range(group):
+            at = columns(j, h)
+            row = cum_ref[j * group + h]
+            cum = columns_of(row, size)
+            to_end = jnp.exp(row[:, length - 1 :] - cum)
+            keys, grads = k_ref[:, at], g_ref[:, at]
+            mixed = (dot(q_ref[:, at], keys, ((1,), (1,))) * decay_matrix(row, size)).astype(BF16)
+            dv = dot(mixed, grads, ((0,), (0,)))
+            dv = dv + to_end * dot(keys, suffix_ref[j * group + h], ((1,), (0,)))
+            dv = dv.astype(BF16)
+            dv_ref[:, at] = dv
+            held[j, pl.ds(0, length), h * size : (h + 1) * size] = dv
+
+    def query_key_part(j):
+        for h in range(group):
+            at = columns(j, h)
+            row = cum_ref[j * group + h]
+            cum = columns_of(row, size)
+            to_end = jnp.exp(row[:, length - 1 :] - cum)
+            keys, grads, values, queries = k_ref[:, at], g_ref[:, at], v_ref[:, at], q_ref[:, at]
+            weighted = dot(grads, values, ((1,), (1,))) * decay_matrix(row, size)
+            weighted = weighted.astype(BF16)
+            qg = dot(weighted, keys, ((1,), (0,)))
+            qg = qg + jnp.exp(cum) * dot(grads, prefix_ref[j * group + h], ((1,), (1,)))
+            kg = dot(weighted, queries, ((0,), (0,)))
+            kg = kg + to_end * dot(values, suffix_ref[j * group + h], ((1,), (1,)))
+            qg_ref[:, at] = qg.astype(BF16)
+            kg_ref[:, at] = kg.astype(BF16)
+
+    def within(j):
+        return (j >= 0) & (j < chunks)
+
+    def line_part(j, way, t):
+        has_source = z > 0 if way == 0 else z < last
+        ahead = t > z if way == 0 else t < z
+
+        @pl.when(has_source)
+        def _():
+            line_copy(j, way, t).wait_recv()
+            slot = t - 1 + way
+            part[j, t] = (part[j, t].astype(F32) + landed[way, slot, j].astype(F32)).astype(BF16)
+
+        @pl.when(ahead)
+        def _():
+            line_copy(j, way, t).start()
+
+    def line_stage(j, way):
+        order = range(last, 0, -1) if way == 0 else range(last)
+        for t in order:
+            reached = z <= t if way == 0 else z >= t
+            pl.when(within(j) & reached)(functools.partial(line_part, j, way, t))
+
+    @pl.loop(0, chunks + 2 + last)
+    def _(i):
+        @pl.when(i < chunks)
+        def _():
+            value_part(i)
+            to_chip(i).start()
+            to_core(i).start()
+
+        @pl.when(within(i - 1))
+        def _():
+            to_chip(i - 1).wait_recv()
+            onward(i - 1).start()
+
+        j = i - 2
+
+        @pl.when(within(j))
+        def _():
+            to_core(j).wait_recv()
+            onward(j).wait_recv()
+            for t in range(last + 1):
+                part[j, t] = dot(
+                    x_ref[t * rows : (t + 1) * rows, :], held[j], ((1,), (0,))
+                ).astype(BF16)
+
+        line_stage(j - z, 0)
+        line_stage(j - last + z, 1)
+
+        @pl.when(within(j))
+        def _():
+            query_key_part(j)
+
+        done = j - last
+
+        @pl.when(within(done))
+        def _():
+            at = pl.ds(pl.multiple_of(done * width, width), width)
+            wg_ref[:, at] = part[done, z]
+
+    @pl.loop(0, chunks)
+    def _(j):
+        to_core(j).wait_send()
+        to_chip(j).wait_send()
+        onward(j).wait_send()
+        for t in range(last + 1):
+            if t > 0:
+                pl.when(t > z)(lambda t=t: line_copy(j, 0, t).wait_send())
+            if t < last:
+                pl.when(t < z)(lambda t=t: line_copy(j, 1, t).wait_send())
+
+
+def mega(blocks, chunks, x_held, queries, keys, values, out_grad, lines, prefix, suffix):
+    length, columns = queries.shape
+    width, planes = columns // chunks, blocks // 4
+    rows = x_held.shape[0] // planes
+    heads, size = prefix.shape[0], prefix.shape[1]
+    vmem = pl.BlockSpec(memory_space=pltpu.VMEM)
+    whole = jax.ShapeDtypeStruct((length, columns), BF16)
+    dma = pltpu.SemaphoreType.DMA
+    return pl.pallas_call(
+        functools.partial(mega_kernel, blocks),
+        out_shape=[whole, whole, whole, jax.ShapeDtypeStruct((rows, columns), BF16)],
+        in_specs=[vmem] * 8,
+        out_specs=[vmem] * 4,
+        scratch_shapes=[
+            pltpu.VMEM((chunks, 4 * length, width), BF16),
+            pltpu.VMEM((chunks, planes, rows, width), BF16),
+            pltpu.VMEM((2, planes - 1, chunks, rows, width), BF16),
+            dma((3, chunks)),
+            dma((3, chunks)),
+            dma((2, planes - 1, chunks)),
+            dma((2, planes - 1, chunks)),
+        ],
+        cost_estimate=pl.CostEstimate(
+            flops=heads * (10 * length * length * size + 8 * length * size * size)
+            + 2 * x_held.size * columns * 4,
+            bytes_accessed=16 * length * columns,
+            transcendentals=2 * heads * length * length,
+        ),
+        compiler_params=pltpu.CompilerParams(
+            collective_id=0, has_side_effects=True, vmem_limit_bytes=60 * 1024 * 1024
+        ),
+    )(x_held, queries, keys, values, out_grad, lines, prefix, suffix)
 
 
 def step(mapping, count):
@@ -228,6 +434,16 @@
     square, state = 2 * length * length * size, 2 * length * size * size
     call = functools.partial(per_head, length=length, size=size)
 
+    if planes and heads % 8 == 0:
+        kv, qd = call(
+            states_kernel, 0, heads, kinds="wwwwl", outs=[("s", BF16)] * 2,
+            flops=2 * state, args=(queries, keys, values, out_grad, lines),
+        )
+        prefix, suffix = plane_scan(kv, qd, totals, index)
+        return mega(
+            blocks, 8, x_held, queries, keys, values, out_grad, lines, prefix, suffix
+        )
+
     states = [
         call(
             states_kernel, i * count, count, kinds="wwwwl", outs=[("s", BF16)] * 2,

time: 365 us -> 319 us (0.87); the launches traced: 359 us -> 318 us
  starting transfers between devices: 110 us -> 6.64 us
  Pallas kernels: 69.4 us -> 158 us
  local copies, waits for them, and re-layouts: 49.1 us -> 36.5 us
  other arithmetic: 23.8 us -> 11.7 us
  matrix products: 8.77 us -> 0 us
  waiting for transfers between devices: 74.3 us -> 81.9 us
    pallas_call x0 -> x1, Pallas kernels: none -> 143 us  [mega(): pl.pallas_call(functools.partial(mega_kernel, blocks), out_shape=[whole,...]
    ppermute x36 -> x0, starting transfers between devices: 76.7 us -> none  [the longest x12 60.4 us: planes_sum(): lax.ppermute(to_up, 'seq', step(lambda i: i + 4 if i // 4 < s else None,...]
    ppermute x36 -> x0, waiting for transfers between devices: 62.9 us -> none  [the longest x12 23.3 us: planes_sum(): lax.ppermute(to_up, 'seq', step(lambda i: i + 4 if i // 4 < s else None,...]
    pallas_call x13 -> x1, Pallas kernels: 69.4 us -> 14.8 us  [per_head(): pl.pallas_call(body, grid=(count,), in_specs=[specs[kind] for kind in kin...]
    ppermute x12 -> x3, waiting for transfers between devices: 1.56 us -> 39 us  [plane_scan(): travelling = lax.ppermute(travelling, 'seq', onward)]
    ppermute x3, waiting for transfers between devices: 0.01 us -> 18.8 us  [plane_rows(): lax.ppermute(columns(place ^ k), 'seq', step(lambda i: i ^ k, 16))]
    ppermute x12 -> x3, starting transfers between devices: 15.8 us -> 3.97 us  [plane_scan(): travelling = lax.ppermute(travelling, 'seq', onward)]
    ppermute x4 -> x1, starting transfers between devices: 9.86 us -> 0.07 us  [plane_scan(): other = lax.ppermute(beyond, 'seq', swap_chip)]
  transfers between devices with their start and end apart: 67 -> 10, of which waited for: 19 -> 7; matrix products, arithmetic and copies ran while one was open for 13% -> 5% of each run, Pallas kernels for 19% -> 0%
where the time goes in v2:
time: 319 us; the launch traced here: 318 us
  Pallas kernels  158 us (50%)
  waiting for transfers between devices  81.9 us (26%)
  local copies, waits for them, and re-layouts  36.5 us (11%)
  blocking collectives  22.6 us (7%)
  other arithmetic  11.7 us (4%)
  starting transfers between devices  6.64 us (2%)
    pallas_call x1, Pallas kernels, mega(): pl.pallas_call(functools.partial(mega_kernel, blocks), out_shape=[whole,...  143 us
    ppermute x3, waiting for transfers between devices, plane_scan(): travelling = lax.ppermute(travelling, 'seq', onward)  39 us
    all_gather x1, blocking collectives, on_device(): totals = lax.all_gather(cumul[-1:], 'seq', axis=0, tiled=True)  22.6 us
    unnamed x43, local copies, waits for them, and re-layouts  21.6 us
    ppermute x3, waiting for transfers between devices, plane_rows(): lax.ppermute(columns(place ^ k), 'seq', step(lambda i: i ^ k, 16))  18.8 us
    pallas_call x1, Pallas kernels, per_head(): pl.pallas_call(body, grid=(count,), in_specs=[specs[kind] for kind in kin...  14.8 us
    ppermute x1, waiting for transfers between devices, plane_scan(): neighbour = lax.ppermute(sent, 'seq', swap_chip).astype(F32)  14.1 us
    ppermute x1, waiting for transfers between devices, plane_scan(): other = lax.ppermute(beyond, 'seq', swap_chip)  9.95 us
  transfers between devices with their start and end apart: 10, of which 7 were waited for; matrix products, arithmetic and copies ran while one was open for 5% of the time, Pallas kernels for 0%

profile of v2, /device:TPU:0, one launch (start us, length us, event | category | flops | bytes accessed | tf_op | source)
XLA Modules:
  0.0 318.5 jit_solution(2694692489083287945)
XLA Ops:
  2.7 1.7 copy-done
  4.4 1.7 copy-done.1
  6.2 1.7 copy-done.2
  7.9 1.7 copy-done.3
  9.7 14.8 %shard_map.93 = (bf16[32,128,128]{2,1,0:T(8,128)(2,1)S(1)}, bf16[32,128,128]{2,1,0:T(8,128)(2,1)S(1)}) custom-call(bf16[320,4096]{1,0:T(8,128)(2,1)S(1)} %copy-done, bf16[320,4096]{1,0:T(8,128)(2,1)S(1)} %copy-done.1, bf16[320,4096]{1,0:T(8,128)(2,1)S(1)} %copy-done.2, bf16[320,4096]{1,0:T(8,128)(2,1)S(1)} %copy-done.3, ...), custom_call_target="tpu_custom_call" | custom-call | flops 671088640 | bytes 18350080 | tf_op jit(solution)/shard_map/pallas_call | solution.py:84
  25.3 22.6 %all-gather = f32[16,1,32]{2,1,0:T(1,128)S(1)} all-gather(f32[1,1,32]{2,1,0:T(1,128)S(1)} %bitcast.96), channel_id=1, replica_groups=mesh['groups'=2,'seq'=16,'heads'=1] {'seq'}, dimensions={0}, use_global_device_ids=true | all-gather | bytes 2176 | tf_op jit(solution)/shard_map/all_gather | solution.py:429
  48.1 1.5 select_convert_fusion.4
  50.0 14.1 %collective-permute-done.4 = bf16[16,128,128]{2,1,0:T(8,128)(2,1)S(1)} collective-permute-done((bf16[16,128,128]{2,1,0:T(8,128)(2,1)S(1)}, bf16[16,128,128]{2,1,0:T(8,128)(2,1)S(1)}, u32[]{:S(2)}, u32[]{:S(2)}) %collective-permute-start.4) | collective-permute-done | bytes 524320 | tf_op jit(solution)/shard_map/ppermute | solution.py:337
  66.3 13.9 %collective-permute-done.5 = bf16[16,128,128]{2,1,0:T(8,128)(2,1)S(1)} collective-permute-done((bf16[16,128,128]{2,1,0:T(8,128)(2,1)S(1)}, bf16[16,128,128]{2,1,0:T(8,128)(2,1)S(1)}, u32[]{:S(2)}, u32[]{:S(2)}) %collective-permute-start.5) | collective-permute-done | bytes 524320 | tf_op jit(solution)/shard_map/ppermute | solution.py:344
  81.5 13.0 %collective-permute-done.6 = bf16[16,128,128]{2,1,0:T(8,128)(2,1)S(1)} collective-permute-done((bf16[16,128,128]{2,1,0:T(8,128)(2,1)S(1)}, bf16[16,128,128]{2,1,0:T(8,128)(2,1)S(1)}, u32[]{:S(2)}, u32[]{:S(2)}) %collective-permute-start.6) | collective-permute-done | bytes 524320 | tf_op jit(solution)/shard_map/ppermute | solution.py:344
  95.9 12.1 %collective-permute-done.7 = bf16[16,128,128]{2,1,0:T(8,128)(2,1)} collective-permute-done((bf16[16,128,128]{2,1,0:T(8,128)(2,1)S(1)}, bf16[16,128,128]{2,1,0:T(8,128)(2,1)}, u32[]{:S(2)}, u32[]{:S(2)}) %collective-permute-start.7) | collective-permute-done | bytes 524320 | tf_op jit(solution)/shard_map/ppermute | solution.py:344
  108.0 1.6 add_convert_fusion
  110.4 9.9 %collective-permute-done.8 = bf16[16,128,128]{2,1,0:T(8,128)(2,1)} collective-permute-done((bf16[16,128,128]{2,1,0:T(8,128)(2,1)S(1)}, bf16[16,128,128]{2,1,0:T(8,128)(2,1)}, u32[]{:S(2)}, u32[]{:S(2)}) %collective-permute-start.8) | collective-permute-done | bytes 524320 | tf_op jit(solution)/shard_map/ppermute | solution.py:349
  120.4 2.4 fusion.9
  124.8 2.9 copy.25
  135.2 11.5 %collective-permute-done.1 = bf16[320,768]{1,0:T(8,128)(2,1)} collective-permute-done((bf16[320,768]{1,0:T(8,128)(2,1)S(1)}, bf16[320,768]{1,0:T(8,128)(2,1)}, u32[]{:S(2)}, u32[]{:S(2)}) %collective-permute-start.1) | collective-permute-done | bytes 491552 | tf_op jit(solution)/shard_map/ppermute | solution.py:392
  148.0 7.3 %collective-permute-done.2 = bf16[320,768]{1,0:T(8,128)(2,1)} collective-permute-done((bf16[320,768]{1,0:T(8,128)(2,1)}, bf16[320,768]{1,0:T(8,128)(2,1)}, u32[]{:S(2)}, u32[]{:S(2)}) %collective-permute-start.2) | collective-permute-done | bytes 491552 | tf_op jit(solution)/shard_map/ppermute | solution.py:392
  155.3 2.1 copy.31
  157.4 4.8 %concatenate.6 = bf16[1280,768]{0,1:T(8,128)(2,1)} concatenate(bf16[320,768]{0,1:T(8,128)(2,1)} %bitcast.90, bf16[320,768]{0,1:T(8,128)(2,1)S(1)} %copy.29, bf16[320,768]{0,1:T(8,128)(2,1)S(1)} %copy.30, bf16[320,768]{0,1:T(8,128)(2,1)} %copy.31), dimensions={0} | concatenate | bytes 3932160 | tf_op jit(solution)/shard_map/concatenate | solution.py:393
  163.8 1.5 fusion.6
  165.3 143.2 %shard_map.94 = (bf16[320,4096]{1,0:T(8,128)(2,1)}, bf16[320,4096]{1,0:T(8,128)(2,1)}, bf16[320,4096]{1,0:T(8,128)(2,1)}, bf16[192,4096]{1,0:T(8,128)(2,1)}) custom-call(bf16[768,1280]{1,0:T(8,128)(2,1)} %bitcast.91, bf16[320,4096]{1,0:T(8,128)(2,1)} %q_ref.3, bf16[320,4096]{1,0:T(8,128)(2,1)} %k_ref.3, bf16[320,4096]{1,0:T(8,128)(2,1)} %v_ref.3, ...), custom_call_target="tpu_custom_call" | custom-call | flops 37748736000 | bytes 20971520 | tf_op jit(solution)/shard_map/pallas_call | solution.py:277
  308.6 3.7 %copy.42 = bf16[320,4096]{1,0:T(8,128)(2,1)} copy(bf16[320,4096]{1,0:T(8,128)(2,1)} %get-tuple-element.33) | data formatting | bytes 5242880
  312.3 1.5 copy.43
  315.0 1.5 copy.44
  (75 shorter events, 24.4 us)
Async XLA Ops:
  2.7 21.9 %copy-start.4 = (f32[32,1,320]{2,1,0:T(1,128)}, f32[32,1,320]{2,1,0:T(1,128)S(1)}, u32[]{:S(2)}) copy-start(f32[32,1,320]{2,1,0:T(1,128)S(1)} %broadcast_in_dim.2.cum_ref) | copy-start | bytes 122884
  2.7 1.8 copy-start
  4.4 1.7 copy-start.1
  24.6 23.4 %collective-permute-start.3 = (bf16[2,16,128,128]{3,2,1,0:T(8,128)(2,1)S(1)}, bf16[2,16,128,128]{3,2,1,0:T(8,128)(2,1)}, u32[]{:S(2)}, u32[]{:S(2)}) collective-permute-start(bf16[2,16,128,128]{3,2,1,0:T(8,128)(2,1)S(1)} %fusion.4), channel_id=1, source_target_pairs={{0,1},{1,0},{2,3},{3,2},{4,5},{5,4},{6,7},{7,6},{8,9},{9,8},{10,11... | collective-permute-start | bytes 3145736 | tf_op jit(solution)/shard_map/ppermute | solution.py:321
  49.6 14.5 %copy-start.5 = (f32[2,16,128,128]{3,2,1,0:T(8,128)}, f32[2,16,128,128]{3,2,1,0:T(8,128)S(1)}, u32[]{:S(2)}) copy-start(f32[2,16,128,128]{3,2,1,0:T(8,128)S(1)} %get-tuple-element.12) | copy-start | bytes 6291460
  49.6 14.5 %copy-start.7 = (f32[2,16,128,128]{3,2,1,0:T(8,128)}, f32[2,16,128,128]{3,2,1,0:T(8,128)S(1)}, u32[]{:S(2)}) copy-start(f32[2,16,128,128]{3,2,1,0:T(8,128)S(1)} %get-tuple-element.13) | copy-start | bytes 6291460
  49.9 14.2 %collective-permute-start.4 = (bf16[16,128,128]{2,1,0:T(8,128)(2,1)S(1)}, bf16[16,128,128]{2,1,0:T(8,128)(2,1)S(1)}, u32[]{:S(2)}, u32[]{:S(2)}) collective-permute-start(bf16[16,128,128]{2,1,0:T(8,128)(2,1)S(1)} %select_convert_fusion.2), channel_id=1, source_target_pairs={{0,2},{1,3},{2,0},{3,1},{4,6},{5,7},{6,4},{7,5},{8,10},{9,11},{10,... | collective-permute-start | bytes 1572872 | tf_op jit(solution)/shard_map/ppermute | solution.py:337
  64.9 55.5 %copy-start.6 = (f32[2,16,128,128]{3,2,1,0:T(8,128)S(1)}, f32[2,16,128,128]{3,2,1,0:T(8,128)}, u32[]{:S(2)}) copy-start(f32[2,16,128,128]{3,2,1,0:T(8,128)} %copy-done.5) | copy-start | bytes 6291460
  64.9 15.3 %collective-permute-start.5 = (bf16[16,128,128]{2,1,0:T(8,128)(2,1)S(1)}, bf16[16,128,128]{2,1,0:T(8,128)(2,1)S(1)}, u32[]{:S(2)}, u32[]{:S(2)}) collective-permute-start(bf16[16,128,128]{2,1,0:T(8,128)(2,1)S(1)} %fusion.1), channel_id=1, source_target_pairs={{2,6},{3,7},{4,0},{5,1},{6,10},{7,11},{8,4},{9,5},{10,14},{11,15},... | collective-permute-start | bytes 1572872 | tf_op jit(solution)/shard_map/ppermute | solution.py:344
  80.2 14.3 %collective-permute-start.6 = (bf16[16,128,128]{2,1,0:T(8,128)(2,1)S(1)}, bf16[16,128,128]{2,1,0:T(8,128)(2,1)S(1)}, u32[]{:S(2)}, u32[]{:S(2)}) collective-permute-start(bf16[16,128,128]{2,1,0:T(8,128)(2,1)S(1)} %collective-permute-done.5), channel_id=1, source_target_pairs={{2,6},{3,7},{4,0},{5,1},{6,10},{7,11},{8,4},{9,5},{10,14},{11,15},... | collective-permute-start | bytes 1572872 | tf_op jit(solution)/shard_map/ppermute | solution.py:344
  94.5 13.5 %copy-start.18 = (bf16[16,128,128]{2,1,0:T(8,128)(2,1)}, bf16[16,128,128]{2,1,0:T(8,128)(2,1)S(1)}, u32[]{:S(2)}) copy-start(bf16[16,128,128]{2,1,0:T(8,128)(2,1)S(1)} %collective-permute-done.6) | copy-start | bytes 1572868
  94.5 13.5 %collective-permute-start.7 = (bf16[16,128,128]{2,1,0:T(8,128)(2,1)S(1)}, bf16[16,128,128]{2,1,0:T(8,128)(2,1)}, u32[]{:S(2)}, u32[]{:S(2)}) collective-permute-start(bf16[16,128,128]{2,1,0:T(8,128)(2,1)S(1)} %collective-permute-done.6), channel_id=1, source_target_pairs={{2,6},{3,7},{4,0},{5,1},{6,10},{7,11},{8,4},{9,5},{10,14},{11,15},... | collective-permute-start | bytes 1572872 | tf_op jit(solution)/shard_map/ppermute | solution.py:344
  109.7 10.7 %collective-permute-start.8 = (bf16[16,128,128]{2,1,0:T(8,128)(2,1)S(1)}, bf16[16,128,128]{2,1,0:T(8,128)(2,1)}, u32[]{:S(2)}, u32[]{:S(2)}) collective-permute-start(bf16[16,128,128]{2,1,0:T(8,128)(2,1)S(1)} %add_convert_fusion), channel_id=1, source_target_pairs={{0,2},{1,3},{2,0},{3,1},{4,6},{5,7},{6,4},{7,5},{8,10},{9,11},{10,... | collective-permute-start | bytes 1572872 | tf_op jit(solution)/shard_map/ppermute | solution.py:349
  122.8 2.0 copy-start.10
  124.8 37.4 %collective-permute-start.9 = (bf16[2,16,128,128]{3,2,1,0:T(8,128)(2,1)}, bf16[2,16,128,128]{3,2,1,0:T(8,128)(2,1)}, u32[]{:S(2)}, u32[]{:S(2)}) collective-permute-start(bf16[2,16,128,128]{3,2,1,0:T(8,128)(2,1)} %select_convert_fusion), channel_id=1, source_target_pairs={{0,1},{1,0},{2,3},{3,2},{4,5},{5,4},{6,7},{7,6},{8,9},{9,8},{10,11... | collective-permute-start | bytes 3145736 | tf_op jit(solution)/shard_map/ppermute | solution.py:359
  129.2 3.6 %copy-start.14 = (bf16[320,4,1,192]{0,3,2,1:T(8,128)(2,1)S(1)}, bf16[320,4,1,192]{0,3,2,1:T(8,128)(2,1)}, u32[]{:S(2)}) copy-start(bf16[320,4,1,192]{0,3,2,1:T(8,128)(2,1)} %get-tuple-element.14) | copy-start | bytes 1474564
  130.6 4.3 %collective-permute-start = (bf16[320,768]{1,0:T(8,128)(2,1)S(1)}, bf16[320,768]{1,0:T(8,128)(2,1)S(1)}, u32[]{:S(2)}, u32[]{:S(2)}) collective-permute-start(bf16[320,768]{1,0:T(8,128)(2,1)S(1)} %copy.26), channel_id=1, source_target_pairs={{0,1},{1,0},{2,3},{3,2},{4,5},{5,4},{6,7},{7,6},{8,9},{9,8},{10,11... | collective-permute-start | bytes 1474568 | tf_op jit(solution)/shard_map/ppermute | solution.py:392
  132.4 14.3 %collective-permute-start.1 = (bf16[320,768]{1,0:T(8,128)(2,1)S(1)}, bf16[320,768]{1,0:T(8,128)(2,1)}, u32[]{:S(2)}, u32[]{:S(2)}) collective-permute-start(bf16[320,768]{1,0:T(8,128)(2,1)S(1)} %copy.27), channel_id=1, source_target_pairs={{0,2},{1,3},{2,0},{3,1},{4,6},{5,7},{6,4},{7,5},{8,10},{9,11},{10,... | collective-permute-start | bytes 1474568 | tf_op jit(solution)/shard_map/ppermute | solution.py:392
  133.8 21.5 %collective-permute-start.2 = (bf16[320,768]{1,0:T(8,128)(2,1)}, bf16[320,768]{1,0:T(8,128)(2,1)}, u32[]{:S(2)}, u32[]{:S(2)}) collective-permute-start(bf16[320,768]{1,0:T(8,128)(2,1)} %copy.28), channel_id=1, source_target_pairs={{0,3},{1,2},{2,1},{3,0},{4,7},{5,6},{6,5},{7,4},{8,11},{9,10},{10,... | collective-permute-start | bytes 1474568 | tf_op jit(solution)/shard_map/ppermute | solution.py:392
  157.4 4.8 %copy-start.9 = (bf16[1,16,128,128]{3,2,1,0:T(8,128)(2,1)S(1)}, bf16[1,16,128,128]{3,2,1,0:T(8,128)(2,1)}, u32[]{:S(2)}) copy-start(bf16[1,16,128,128]{3,2,1,0:T(8,128)(2,1)} %copy-done.8) | copy-start | bytes 1572868
  157.4 4.8 %copy-start.11 = (bf16[1,16,128,128]{3,2,1,0:T(8,128)(2,1)S(1)}, bf16[1,16,128,128]{3,2,1,0:T(8,128)(2,1)}, u32[]{:S(2)}) copy-start(bf16[1,16,128,128]{3,2,1,0:T(8,128)(2,1)} %copy-done.10) | copy-start | bytes 1572868
  308.6 3.7 %copy-start.13 = (bf16[320,4096]{1,0:T(8,128)(2,1)S(1)}, bf16[320,4096]{1,0:T(8,128)(2,1)}, u32[]{:S(2)}) copy-start(bf16[320,4096]{1,0:T(8,128)(2,1)} %get-tuple-element.34) | copy-start | bytes 7864324
  312.3 2.7 copy-start.12
  315.0 2.4 copy-start.17
  (5 other events, 5.9 us)

commit v3 on v2

--- a/solution.py
+++ b/solution.py
@@ -390,6 +390,10 @@
     held = [columns(place)]
     for k in (1, 2, 3):
         held.append(lax.ppermute(columns(place ^ k), "seq", step(lambda i: i ^ k, 16)))
+    return held
+
+
+def laid_out(held):
     return jnp.concatenate(held, axis=0).T
 
 
@@ -439,9 +443,10 @@
             states_kernel, 0, heads, kinds="wwwwl", outs=[("s", BF16)] * 2,
             flops=2 * state, args=(queries, keys, values, out_grad, lines),
         )
+        kv, qd, x_held = lax.optimization_barrier((kv, qd, x_held))
         prefix, suffix = plane_scan(kv, qd, totals, index)
         return mega(
-            blocks, 8, x_held, queries, keys, values, out_grad, lines, prefix, suffix
+            blocks, 16 if heads % 16 == 0 else 8, laid_out(x_held), queries, keys, values, out_grad, lines, prefix, suffix
         )
 
     states = [
@@ -471,7 +476,7 @@
         )
         value_grads.append(dv)
         if planes:
-            part = dot(x_held, plane_values(dv), ((1,), (0,))).astype(BF16)
+            part = dot(laid_out(x_held), plane_values(dv), ((1,), (0,))).astype(BF16)
             part = part.reshape(4, part.shape[0] // 4, part.shape[1])
             sums.append(planes_sum(part, index))
         else:

time: 319 us -> 288 us (0.903)
  waiting for transfers between devices: 81.9 us -> 63.1 us
  Pallas kernels: 158 us -> 146 us
    ppermute x3, waiting for transfers between devices: 18.8 us -> 0.01 us  [plane_rows(): lax.ppermute(columns(place ^ k), 'seq', step(lambda i: i ^ k, 16))]
    pallas_call x1, Pallas kernels: 143 us -> 131 us  [mega(): pl.pallas_call(functools.partial(mega_kernel, blocks), out_shape=[whole,...]
    optimization_barrier x0 -> x3, local copies, waits for them, and re-layouts: none -> 4.22 us  [on_device(): kv, qd, x_held = lax.optimization_barrier((kv, qd, x_held))]
    ppermute x3 -> x0, local copies, waits for them, and re-layouts: 3.72 us -> none  [plane_rows(): lax.ppermute(columns(place ^ k), 'seq', step(lambda i: i ^ k, 16))]
    unnamed x43 -> x51, local copies, waits for them, and re-layouts: 21.6 us -> 22.6 us
  transfers between devices with their start and end apart: 10 -> 10, of which waited for: 7 -> 5; matrix products, arithmetic and copies ran while one was open for 5% -> 4% of each run, Pallas kernels for 0% -> 5%
where the time goes in v3:
time: 288 us
  Pallas kernels  146 us (51%)
  waiting for transfers between devices  63.1 us (22%)
  local copies, waits for them, and re-layouts  37.7 us (13%)
  blocking collectives  21.9 us (8%)
  other arithmetic  10.5 us (4%)
  starting transfers between devices  7.38 us (3%)
    pallas_call x1, Pallas kernels, mega(): pl.pallas_call(functools.partial(mega_kernel, blocks), out_shape=[whole,...  131 us
    ppermute x3, waiting for transfers between devices, plane_scan(): travelling = lax.ppermute(travelling, 'seq', onward)  39 us
    unnamed x51, local copies, waits for them, and re-layouts  22.6 us
    all_gather x1, blocking collectives, on_device(): totals = lax.all_gather(cumul[-1:], 'seq', axis=0, tiled=True)  21.9 us
    pallas_call x1, Pallas kernels, per_head(): pl.pallas_call(body, grid=(count,), in_specs=[specs[kind] for kind in kin...  14.8 us
    ppermute x1, waiting for transfers between devices, plane_scan(): neighbour = lax.ppermute(sent, 'seq', swap_chip).astype(F32)  14.1 us
    ppermute x1, waiting for transfers between devices, plane_scan(): other = lax.ppermute(beyond, 'seq', swap_chip)  9.93 us
  transfers between devices with their start and end apart: 10, of which 5 were waited for; matrix products, arithmetic and copies ran while one was open for 4% of the time, Pallas kernels for 5%

profile of v3, /device:TPU:0, one launch (start us, length us, event | category | flops | bytes accessed | tf_op | source)
XLA Modules:
  0.0 287.6 jit_solution(14430199099221165690)
XLA Ops:
  0.7 2.9 %copy.27 = bf16[320,3072]{0,1:T(8,128)(2,1)S(1)} copy(bf16[320,3072]{1,0:T(8,128)(2,1)} %param.6) | data formatting | bytes 3932160 | tf_op args[0]
  4.9 2.1 copy.28
  8.4 2.5 collective-permute-start.1
  13.4 1.7 copy-done
  15.1 1.7 copy-done.1
  16.8 1.7 copy-done.2
  18.6 1.7 copy-done.3
  20.3 14.8 %shard_map.93 = (bf16[32,128,128]{2,1,0:T(8,128)(2,1)S(1)}, bf16[32,128,128]{2,1,0:T(8,128)(2,1)S(1)}) custom-call(bf16[320,4096]{1,0:T(8,128)(2,1)S(1)} %copy-done, bf16[320,4096]{1,0:T(8,128)(2,1)S(1)} %copy-done.1, bf16[320,4096]{1,0:T(8,128)(2,1)S(1)} %copy-done.2, bf16[320,4096]{1,0:T(8,128)(2,1)S(1)} %copy-done.3, ...), custom_call_target="tpu_custom_call" | custom-call | flops 671088640 | bytes 18350080 | tf_op jit(solution)/shard_map/pallas_call | solution.py:84
  36.6 21.9 %all-gather = f32[16,1,32]{2,1,0:T(1,128)S(1)} all-gather(f32[1,1,32]{2,1,0:T(1,128)S(1)} %bitcast.96), channel_id=1, replica_groups=mesh['groups'=2,'seq'=16,'heads'=1] {'seq'}, dimensions={0}, use_global_device_ids=true | all-gather | bytes 2176 | tf_op jit(solution)/shard_map/all_gather | solution.py:433
  58.7 1.5 select_convert_fusion.4
  60.6 14.1 %collective-permute-done.4 = bf16[16,128,128]{2,1,0:T(8,128)(2,1)S(1)} collective-permute-done((bf16[16,128,128]{2,1,0:T(8,128)(2,1)S(1)}, bf16[16,128,128]{2,1,0:T(8,128)(2,1)S(1)}, u32[]{:S(2)}, u32[]{:S(2)}) %collective-permute-start.4) | collective-permute-done | bytes 524320 | tf_op jit(solution)/shard_map/ppermute | solution.py:337
  76.9 13.9 %collective-permute-done.5 = bf16[16,128,128]{2,1,0:T(8,128)(2,1)S(1)} collective-permute-done((bf16[16,128,128]{2,1,0:T(8,128)(2,1)S(1)}, bf16[16,128,128]{2,1,0:T(8,128)(2,1)S(1)}, u32[]{:S(2)}, u32[]{:S(2)}) %collective-permute-start.5) | collective-permute-done | bytes 524320 | tf_op jit(solution)/shard_map/ppermute | solution.py:344
  92.2 13.0 %collective-permute-done.6 = bf16[16,128,128]{2,1,0:T(8,128)(2,1)S(1)} collective-permute-done((bf16[16,128,128]{2,1,0:T(8,128)(2,1)S(1)}, bf16[16,128,128]{2,1,0:T(8,128)(2,1)S(1)}, u32[]{:S(2)}, u32[]{:S(2)}) %collective-permute-start.6) | collective-permute-done | bytes 524320 | tf_op jit(solution)/shard_map/ppermute | solution.py:344
  106.5 12.1 %collective-permute-done.7 = bf16[16,128,128]{2,1,0:T(8,128)(2,1)} collective-permute-done((bf16[16,128,128]{2,1,0:T(8,128)(2,1)S(1)}, bf16[16,128,128]{2,1,0:T(8,128)(2,1)}, u32[]{:S(2)}, u32[]{:S(2)}) %collective-permute-start.7) | collective-permute-done | bytes 524320 | tf_op jit(solution)/shard_map/ppermute | solution.py:344
  118.6 1.6 add_convert_fusion
  121.1 9.9 %collective-permute-done.8 = bf16[16,128,128]{2,1,0:T(8,128)(2,1)} collective-permute-done((bf16[16,128,128]{2,1,0:T(8,128)(2,1)S(1)}, bf16[16,128,128]{2,1,0:T(8,128)(2,1)}, u32[]{:S(2)}, u32[]{:S(2)}) %collective-permute-start.8) | collective-permute-done | bytes 524320 | tf_op jit(solution)/shard_map/ppermute | solution.py:349
  131.0 2.4 fusion.9
  135.4 2.1 copy.31
  139.7 5.1 %concatenate.6 = bf16[1280,768]{0,1:T(8,128)(2,1)} concatenate(bf16[320,768]{0,1:T(8,128)(2,1)} %bitcast.90, bf16[320,768]{0,1:T(8,128)(2,1)} %copy.31, bf16[320,768]{0,1:T(8,128)(2,1)} %copy.32, bf16[320,768]{0,1:T(8,128)(2,1)} %copy.33), dimensions={0} | concatenate | bytes 3932160 | tf_op jit(solution)/shard_map/concatenate | solution.py:397
  145.1 1.5 fusion.6
  146.6 131.2 %shard_map.94 = (bf16[320,4096]{1,0:T(8,128)(2,1)}, bf16[320,4096]{1,0:T(8,128)(2,1)}, bf16[320,4096]{1,0:T(8,128)(2,1)}, bf16[192,4096]{1,0:T(8,128)(2,1)}) custom-call(bf16[768,1280]{1,0:T(8,128)(2,1)} %bitcast.91, bf16[320,4096]{1,0:T(8,128)(2,1)} %q_ref.3, bf16[320,4096]{1,0:T(8,128)(2,1)} %k_ref.3, bf16[320,4096]{1,0:T(8,128)(2,1)} %v_ref.3, ...), custom_call_target="tpu_custom_call" | custom-call | flops 37748736000 | bytes 20971520 | tf_op jit(solution)/shard_map/pallas_call | solution.py:277
  277.8 3.7 %copy.42 = bf16[320,4096]{1,0:T(8,128)(2,1)} copy(bf16[320,4096]{1,0:T(8,128)(2,1)} %get-tuple-element.45) | data formatting | bytes 5242880
  281.5 1.5 copy.43
  284.1 1.5 copy.44
  (83 shorter events, 20.2 us)
Async XLA Ops:
  4.9 7.2 %copy-start.22 = (f32[320,32]{0,1:T(8,128)S(1)}, f32[320,32]{0,1:T(8,128)}, u32[]{:S(2)}) copy-start(f32[320,32]{0,1:T(8,128)} %param.11) | copy-start | bytes 122884
  7.0 28.2 %collective-permute-start = (bf16[320,768]{1,0:T(8,128)(2,1)}, bf16[320,768]{1,0:T(8,128)(2,1)}, u32[]{:S(2)}, u32[]{:S(2)}) collective-permute-start(bf16[320,768]{1,0:T(8,128)(2,1)} %copy.28), channel_id=1, source_target_pairs={{0,1},{1,0},{2,3},{3,2},{4,5},{5,4},{6,7},{7,6},{8,9},{9,8},{10,11... | collective-permute-start | bytes 1474568 | tf_op jit(solution)/shard_map/ppermute | solution.py:392
  8.4 26.8 %collective-permute-start.1 = (bf16[320,768]{1,0:T(8,128)(2,1)}, bf16[320,768]{1,0:T(8,128)(2,1)S(1)}, u32[]{:S(2)}, u32[]{:S(2)}) collective-permute-start(bf16[320,768]{1,0:T(8,128)(2,1)} %copy.29), channel_id=1, source_target_pairs={{0,2},{1,3},{2,0},{3,1},{4,6},{5,7},{6,4},{7,5},{8,10},{9,11},{10,... | collective-permute-start | bytes 1474568 | tf_op jit(solution)/shard_map/ppermute | solution.py:392
  12.0 23.2 %collective-permute-start.2 = (bf16[320,768]{1,0:T(8,128)(2,1)}, bf16[320,768]{1,0:T(8,128)(2,1)S(1)}, u32[]{:S(2)}, u32[]{:S(2)}) collective-permute-start(bf16[320,768]{1,0:T(8,128)(2,1)} %copy.30), channel_id=1, source_target_pairs={{0,3},{1,2},{2,1},{3,0},{4,7},{5,6},{6,5},{7,4},{8,11},{9,10},{10,... | collective-permute-start | bytes 1474568 | tf_op jit(solution)/shard_map/ppermute | solution.py:392
  13.3 21.8 %copy-start.4 = (f32[32,1,320]{2,1,0:T(1,128)}, f32[32,1,320]{2,1,0:T(1,128)S(1)}, u32[]{:S(2)}) copy-start(f32[32,1,320]{2,1,0:T(1,128)S(1)} %broadcast_in_dim.2.cum_ref) | copy-start | bytes 122884
  36.3 22.4 %collective-permute-start.3 = (bf16[2,16,128,128]{3,2,1,0:T(8,128)(2,1)S(1)}, bf16[2,16,128,128]{3,2,1,0:T(8,128)(2,1)}, u32[]{:S(2)}, u32[]{:S(2)}) collective-permute-start(bf16[2,16,128,128]{3,2,1,0:T(8,128)(2,1)S(1)} %fusion.4), channel_id=1, source_target_pairs={{0,1},{1,0},{2,3},{3,2},{4,5},{5,4},{6,7},{7,6},{8,9},{9,8},{10,11... | collective-permute-start | bytes 3145736 | tf_op jit(solution)/shard_map/ppermute | solution.py:321
  60.2 14.5 %copy-start.5 = (f32[2,16,128,128]{3,2,1,0:T(8,128)}, f32[2,16,128,128]{3,2,1,0:T(8,128)S(1)}, u32[]{:S(2)}) copy-start(f32[2,16,128,128]{3,2,1,0:T(8,128)S(1)} %get-tuple-element.24) | copy-start | bytes 6291460
  60.2 14.5 %copy-start.7 = (f32[2,16,128,128]{3,2,1,0:T(8,128)}, f32[2,16,128,128]{3,2,1,0:T(8,128)S(1)}, u32[]{:S(2)}) copy-start(f32[2,16,128,128]{3,2,1,0:T(8,128)S(1)} %get-tuple-element.25) | copy-start | bytes 6291460
  60.5 14.2 %collective-permute-start.4 = (bf16[16,128,128]{2,1,0:T(8,128)(2,1)S(1)}, bf16[16,128,128]{2,1,0:T(8,128)(2,1)S(1)}, u32[]{:S(2)}, u32[]{:S(2)}) collective-permute-start(bf16[16,128,128]{2,1,0:T(8,128)(2,1)S(1)} %select_convert_fusion.2), channel_id=1, source_target_pairs={{0,2},{1,3},{2,0},{3,1},{4,6},{5,7},{6,4},{7,5},{8,10},{9,11},{10,... | collective-permute-start | bytes 1572872 | tf_op jit(solution)/shard_map/ppermute | solution.py:337
  75.5 55.5 %copy-start.6 = (f32[2,16,128,128]{3,2,1,0:T(8,128)S(1)}, f32[2,16,128,128]{3,2,1,0:T(8,128)}, u32[]{:S(2)}) copy-start(f32[2,16,128,128]{3,2,1,0:T(8,128)} %copy-done.5) | copy-start | bytes 6291460
  75.5 15.3 %collective-permute-start.5 = (bf16[16,128,128]{2,1,0:T(8,128)(2,1)S(1)}, bf16[16,128,128]{2,1,0:T(8,128)(2,1)S(1)}, u32[]{:S(2)}, u32[]{:S(2)}) collective-permute-start(bf16[16,128,128]{2,1,0:T(8,128)(2,1)S(1)} %fusion.1), channel_id=1, source_target_pairs={{2,6},{3,7},{4,0},{5,1},{6,10},{7,11},{8,4},{9,5},{10,14},{11,15},... | collective-permute-start | bytes 1572872 | tf_op jit(solution)/shard_map/ppermute | solution.py:344
  90.9 14.3 %collective-permute-start.6 = (bf16[16,128,128]{2,1,0:T(8,128)(2,1)S(1)}, bf16[16,128,128]{2,1,0:T(8,128)(2,1)S(1)}, u32[]{:S(2)}, u32[]{:S(2)}) collective-permute-start(bf16[16,128,128]{2,1,0:T(8,128)(2,1)S(1)} %collective-permute-done.5), channel_id=1, source_target_pairs={{2,6},{3,7},{4,0},{5,1},{6,10},{7,11},{8,4},{9,5},{10,14},{11,15},... | collective-permute-start | bytes 1572872 | tf_op jit(solution)/shard_map/ppermute | solution.py:344
  105.2 13.5 %copy-start.17 = (bf16[16,128,128]{2,1,0:T(8,128)(2,1)}, bf16[16,128,128]{2,1,0:T(8,128)(2,1)S(1)}, u32[]{:S(2)}) copy-start(bf16[16,128,128]{2,1,0:T(8,128)(2,1)S(1)} %collective-permute-done.6) | copy-start | bytes 1572868
  105.2 13.5 %collective-permute-start.7 = (bf16[16,128,128]{2,1,0:T(8,128)(2,1)S(1)}, bf16[16,128,128]{2,1,0:T(8,128)(2,1)}, u32[]{:S(2)}, u32[]{:S(2)}) collective-permute-start(bf16[16,128,128]{2,1,0:T(8,128)(2,1)S(1)} %collective-permute-done.6), channel_id=1, source_target_pairs={{2,6},{3,7},{4,0},{5,1},{6,10},{7,11},{8,4},{9,5},{10,14},{11,15},... | collective-permute-start | bytes 1572872 | tf_op jit(solution)/shard_map/ppermute | solution.py:344
  120.3 10.7 %collective-permute-start.8 = (bf16[16,128,128]{2,1,0:T(8,128)(2,1)S(1)}, bf16[16,128,128]{2,1,0:T(8,128)(2,1)}, u32[]{:S(2)}, u32[]{:S(2)}) collective-permute-start(bf16[16,128,128]{2,1,0:T(8,128)(2,1)S(1)} %add_convert_fusion), channel_id=1, source_target_pairs={{0,2},{1,3},{2,0},{3,1},{4,6},{5,7},{6,4},{7,5},{8,10},{9,11},{10,... | collective-permute-start | bytes 1572872 | tf_op jit(solution)/shard_map/ppermute | solution.py:349
  133.4 2.0 copy-start.10
  134.3 3.2 %copy-start.19 = (bf16[320,768]{1,0:T(8,128)(2,1)S(1)}, bf16[320,768]{1,0:T(8,128)(2,1)}, u32[]{:S(2)}) copy-start(bf16[320,768]{1,0:T(8,128)(2,1)} %copy-done.18) | copy-start | bytes 1474564
  134.3 4.3 %copy-start.21 = (bf16[320,768]{1,0:T(8,128)(2,1)S(1)}, bf16[320,768]{1,0:T(8,128)(2,1)}, u32[]{:S(2)}) copy-start(bf16[320,768]{1,0:T(8,128)(2,1)} %copy-done.20) | copy-start | bytes 1474564
  135.4 9.3 %collective-permute-start.9 = (bf16[2,16,128,128]{3,2,1,0:T(8,128)(2,1)}, bf16[2,16,128,128]{3,2,1,0:T(8,128)(2,1)S(1)}, u32[]{:S(2)}, u32[]{:S(2)}) collective-permute-start(bf16[2,16,128,128]{3,2,1,0:T(8,128)(2,1)} %select_convert_fusion), channel_id=1, source_target_pairs={{0,1},{1,0},{2,3},{3,2},{4,5},{5,4},{6,7},{7,6},{8,9},{9,8},{10,11... | collective-permute-start | bytes 3145736 | tf_op jit(solution)/shard_map/ppermute | solution.py:359
  139.6 5.1 %copy-start.9 = (bf16[1,16,128,128]{3,2,1,0:T(8,128)(2,1)S(1)}, bf16[1,16,128,128]{3,2,1,0:T(8,128)(2,1)}, u32[]{:S(2)}) copy-start(bf16[1,16,128,128]{3,2,1,0:T(8,128)(2,1)} %copy-done.8) | copy-start | bytes 1572868
  139.6 5.1 %copy-start.11 = (bf16[1,16,128,128]{3,2,1,0:T(8,128)(2,1)S(1)}, bf16[1,16,128,128]{3,2,1,0:T(8,128)(2,1)}, u32[]{:S(2)}) copy-start(bf16[1,16,128,128]{3,2,1,0:T(8,128)(2,1)} %copy-done.10) | copy-start | bytes 1572868
  277.8 3.7 %copy-start.13 = (bf16[320,4096]{1,0:T(8,128)(2,1)S(1)}, bf16[320,4096]{1,0:T(8,128)(2,1)}, u32[]{:S(2)}) copy-start(bf16[320,4096]{1,0:T(8,128)(2,1)} %get-tuple-element.46) | copy-start | bytes 7864324
  281.5 2.7 copy-start.12
  284.1 2.4 copy-start.16
  (9 other events, 11.1 us)

commit v4 on v3

--- a/solution.py
+++ b/solution.py
@@ -444,7 +444,12 @@
             flops=2 * state, args=(queries, keys, values, out_grad, lines),
         )
         kv, qd, x_held = lax.optimization_barrier((kv, qd, x_held))
-        prefix, suffix = plane_scan(kv, qd, totals, index)
+        cut = heads // 2
+        scans = [
+            plane_scan(kv[own], qd[own], totals[:, own], index)
+            for own in (slice(0, cut), slice(cut, heads))
+        ]
+        prefix, suffix = (jnp.concatenate(halves) for halves in zip(*scans))
         return mega(
             blocks, 16 if heads % 16 == 0 else 8, laid_out(x_held), queries, keys, values, out_grad, lines, prefix, suffix
         )

time: 288 us -> 286 us (level)
  waiting for transfers between devices: 63.1 us -> 38.6 us
  blocking collectives: 21.9 us -> 35 us
  starting transfers between devices: 7.38 us -> 13.8 us
  other arithmetic: 10.5 us -> 14.3 us
    ppermute x3 -> x6, waiting for transfers between devices: 39 us -> 24.1 us  [plane_scan(): travelling = lax.ppermute(travelling, 'seq', onward)]
    all_gather x1, blocking collectives: 21.9 us -> 35 us  [on_device(): totals = lax.all_gather(cumul[-1:], 'seq', axis=0, tiled=True)]
    ppermute x1 -> x2, waiting for transfers between devices: 9.93 us -> 2.64 us  [plane_scan(): other = lax.ppermute(beyond, 'seq', swap_chip)]
    ppermute x1 -> x2, waiting for transfers between devices: 14.1 us -> 10.1 us  [plane_scan(): neighbour = lax.ppermute(sent, 'seq', swap_chip).astype(F32)]
    ppermute x3 -> x6, starting transfers between devices: 3.97 us -> 7.71 us  [plane_scan(): travelling = lax.ppermute(travelling, 'seq', onward)]
    unnamed x51, local copies, waits for them, and re-layouts: 22.6 us -> 19.4 us
  transfers between devices with their start and end apart: 10 -> 17, of which waited for: 5 -> 12; matrix products, arithmetic and copies ran while one was open for 4% -> 9% of each run, Pallas kernels for 5% -> 5%
where the time goes in v4:
time: 286 us; the launch traced here: 285 us
  Pallas kernels  146 us (51%)
  waiting for transfers between devices  38.6 us (13%)
  local copies, waits for them, and re-layouts  36.1 us (13%)
  blocking collectives  35 us (12%)
  other arithmetic  14.3 us (5%)
  starting transfers between devices  13.8 us (5%)
    pallas_call x1, Pallas kernels, mega(): pl.pallas_call(functools.partial(mega_kernel, blocks), out_shape=[whole,...  131 us
    all_gather x1, blocking collectives, on_device(): totals = lax.all_gather(cumul[-1:], 'seq', axis=0, tiled=True)  35 us
    ppermute x6, waiting for transfers between devices, plane_scan(): travelling = lax.ppermute(travelling, 'seq', onward)  24.1 us
    unnamed x51, local copies, waits for them, and re-layouts  19.4 us
    pallas_call x1, Pallas kernels, per_head(): pl.pallas_call(body, grid=(count,), in_specs=[specs[kind] for kind in kin...  14.8 us
    ppermute x2, waiting for transfers between devices, plane_scan(): neighbour = lax.ppermute(sent, 'seq', swap_chip).astype(F32)  10.1 us
    ppermute x6, starting transfers between devices, plane_scan(): travelling = lax.ppermute(travelling, 'seq', onward)  7.71 us
  transfers between devices with their start and end apart: 17, of which 12 were waited for; matrix products, arithmetic and copies ran while one was open for 9% of the time, Pallas kernels for 5%

profile of v4, /device:TPU:0, one launch (start us, length us, event | category | flops | bytes accessed | tf_op | source)
XLA Modules:
  0.0 284.8 jit_solution(16445349109713769198)
XLA Ops:
  0.7 2.9 %copy.27 = bf16[320,3072]{0,1:T(8,128)(2,1)S(1)} copy(bf16[320,3072]{1,0:T(8,128)(2,1)} %param.6) | data formatting | bytes 3932160 | tf_op args[0]
  4.9 2.2 copy.28
  7.5 2.1 copy.29
  9.6 2.5 collective-permute-start.1
  14.6 35.0 %all-gather = f32[16,1,32]{2,1,0:T(1,128)S(1)} all-gather(f32[1,1,32]{2,1,0:T(1,128)S(1)} %bitcast.159), channel_id=1, replica_groups=mesh['groups'=2,'seq'=16,'heads'=1] {'seq'}, dimensions={0}, use_global_device_ids=true | all-gather | bytes 2176 | tf_op jit(solution)/shard_map/all_gather | solution.py:433
  50.5 1.7 copy-done.1
  52.2 1.7 copy-done.2
  53.9 1.7 copy-done.3
  55.7 14.8 %shard_map.93 = (bf16[32,128,128]{2,1,0:T(8,128)(2,1)S(1)}, bf16[32,128,128]{2,1,0:T(8,128)(2,1)S(1)}) custom-call(bf16[320,4096]{1,0:T(8,128)(2,1)S(1)} %copy-done, bf16[320,4096]{1,0:T(8,128)(2,1)S(1)} %copy-done.1, bf16[320,4096]{1,0:T(8,128)(2,1)S(1)} %copy-done.2, bf16[320,4096]{1,0:T(8,128)(2,1)S(1)} %copy-done.3, ...), custom_call_target="tpu_custom_call" | custom-call | flops 671088640 | bytes 18350080 | tf_op jit(solution)/shard_map/pallas_call | solution.py:84
  74.3 1.8 collective-permute-start.4
  76.1 6.7 %collective-permute-done.11 = bf16[8,128,128]{2,1,0:T(8,128)(2,1)S(1)} collective-permute-done((bf16[8,128,128]{2,1,0:T(8,128)(2,1)S(1)}, bf16[8,128,128]{2,1,0:T(8,128)(2,1)S(1)}, u32[]{:S(2)}, u32[]{:S(2)}) %collective-permute-start.11) | collective-permute-done | bytes 262176 | tf_op jit(solution)/shard_map/ppermute | solution.py:337
  84.4 3.4 %collective-permute-done.4 = bf16[8,128,128]{2,1,0:T(8,128)(2,1)S(1)} collective-permute-done((bf16[8,128,128]{2,1,0:T(8,128)(2,1)S(1)}, bf16[8,128,128]{2,1,0:T(8,128)(2,1)S(1)}, u32[]{:S(2)}, u32[]{:S(2)}) %collective-permute-start.4) | collective-permute-done | bytes 262176 | tf_op jit(solution)/shard_map/ppermute | solution.py:337
  90.1 2.0 collective-permute-done.12
  93.4 6.6 %collective-permute-done.5 = bf16[8,128,128]{2,1,0:T(8,128)(2,1)S(1)} collective-permute-done((bf16[8,128,128]{2,1,0:T(8,128)(2,1)S(1)}, bf16[8,128,128]{2,1,0:T(8,128)(2,1)S(1)}, u32[]{:S(2)}, u32[]{:S(2)}) %collective-permute-start.5) | collective-permute-done | bytes 262176 | tf_op jit(solution)/shard_map/ppermute | solution.py:344
  101.2 4.4 %collective-permute-done.13 = bf16[8,128,128]{2,1,0:T(8,128)(2,1)} collective-permute-done((bf16[8,128,128]{2,1,0:T(8,128)(2,1)S(1)}, bf16[8,128,128]{2,1,0:T(8,128)(2,1)}, u32[]{:S(2)}, u32[]{:S(2)}) %collective-permute-start.13) | collective-permute-done | bytes 262176 | tf_op jit(solution)/shard_map/ppermute | solution.py:344
  107.0 4.2 %collective-permute-done.6 = bf16[8,128,128]{2,1,0:T(8,128)(2,1)} collective-permute-done((bf16[8,128,128]{2,1,0:T(8,128)(2,1)S(1)}, bf16[8,128,128]{2,1,0:T(8,128)(2,1)}, u32[]{:S(2)}, u32[]{:S(2)}) %collective-permute-start.6) | collective-permute-done | bytes 262176 | tf_op jit(solution)/shard_map/ppermute | solution.py:344
  112.6 4.5 %collective-permute-done.14 = bf16[8,128,128]{2,1,0:T(8,128)(2,1)} collective-permute-done((bf16[8,128,128]{2,1,0:T(8,128)(2,1)}, bf16[8,128,128]{2,1,0:T(8,128)(2,1)}, u32[]{:S(2)}, u32[]{:S(2)}) %collective-permute-start.14) | collective-permute-done | bytes 262176 | tf_op jit(solution)/shard_map/ppermute | solution.py:344
  118.6 2.4 collective-permute-done.7
  121.0 2.0 add_convert_fusion.1
  123.0 2.6 collective-permute-done.15
  131.1 2.1 copy.33
  133.2 4.7 %concatenate.15 = bf16[1280,768]{0,1:T(8,128)(2,1)} concatenate(bf16[320,768]{0,1:T(8,128)(2,1)} %bitcast.150, bf16[320,768]{0,1:T(8,128)(2,1)S(1)} %copy.31, bf16[320,768]{0,1:T(8,128)(2,1)S(1)} %copy.32, bf16[320,768]{0,1:T(8,128)(2,1)} %copy.33), dimensions={0} | concatenate | bytes 3932160 | tf_op jit(solution)/shard_map/concatenate | solution.py:397
  144.1 130.9 %shard_map.94 = (bf16[320,4096]{1,0:T(8,128)(2,1)}, bf16[320,4096]{1,0:T(8,128)(2,1)}, bf16[320,4096]{1,0:T(8,128)(2,1)}, bf16[192,4096]{1,0:T(8,128)(2,1)}) custom-call(bf16[768,1280]{1,0:T(8,128)(2,1)} %bitcast.151, bf16[320,4096]{1,0:T(8,128)(2,1)} %q_ref.3, bf16[320,4096]{1,0:T(8,128)(2,1)} %k_ref.3, bf16[320,4096]{1,0:T(8,128)(2,1)} %v_ref.3, ...), custom_call_target="tpu_custom_call" | custom-call | flops 37748736000 | bytes 20971520 | tf_op jit(solution)/shard_map/pallas_call | solution.py:277
  275.0 3.7 %copy.42 = bf16[320,4096]{1,0:T(8,128)(2,1)} copy(bf16[320,4096]{1,0:T(8,128)(2,1)} %get-tuple-element.72) | data formatting | bytes 5242880
  (117 shorter events, 36.9 us)
Async XLA Ops:
  4.9 8.4 %copy-start.21 = (f32[320,32]{0,1:T(8,128)S(1)}, f32[320,32]{0,1:T(8,128)}, u32[]{:S(2)}) copy-start(f32[320,32]{0,1:T(8,128)} %param.11) | copy-start | bytes 122884
  4.9 45.6 %copy-start = (bf16[320,4096]{1,0:T(8,128)(2,1)S(1)}, bf16[320,4096]{1,0:T(8,128)(2,1)}, u32[]{:S(2)}) copy-start(bf16[320,4096]{1,0:T(8,128)(2,1)} %q_ref.3) | copy-start | bytes 7864324
  7.1 63.4 %collective-permute-start = (bf16[320,768]{1,0:T(8,128)(2,1)}, bf16[320,768]{1,0:T(8,128)(2,1)}, u32[]{:S(2)}, u32[]{:S(2)}) collective-permute-start(bf16[320,768]{1,0:T(8,128)(2,1)} %copy.28), channel_id=1, source_target_pairs={{0,1},{1,0},{2,3},{3,2},{4,5},{5,4},{6,7},{7,6},{8,9},{9,8},{10,11... | collective-permute-start | bytes 1474568 | tf_op jit(solution)/shard_map/ppermute | solution.py:392
  9.6 60.9 %collective-permute-start.1 = (bf16[320,768]{1,0:T(8,128)(2,1)}, bf16[320,768]{1,0:T(8,128)(2,1)}, u32[]{:S(2)}, u32[]{:S(2)}) collective-permute-start(bf16[320,768]{1,0:T(8,128)(2,1)} %copy.29), channel_id=1, source_target_pairs={{0,2},{1,3},{2,0},{3,1},{4,6},{5,7},{6,4},{7,5},{8,10},{9,11},{10,... | collective-permute-start | bytes 1474568 | tf_op jit(solution)/shard_map/ppermute | solution.py:392
  13.1 57.4 %collective-permute-start.2 = (bf16[320,768]{1,0:T(8,128)(2,1)}, bf16[320,768]{1,0:T(8,128)(2,1)S(1)}, u32[]{:S(2)}, u32[]{:S(2)}) collective-permute-start(bf16[320,768]{1,0:T(8,128)(2,1)} %copy.30), channel_id=1, source_target_pairs={{0,3},{1,2},{2,1},{3,0},{4,7},{5,6},{6,5},{7,4},{8,11},{9,10},{10,... | collective-permute-start | bytes 1474568 | tf_op jit(solution)/shard_map/ppermute | solution.py:392
  49.7 20.8 %copy-start.4 = (f32[32,1,320]{2,1,0:T(1,128)}, f32[32,1,320]{2,1,0:T(1,128)S(1)}, u32[]{:S(2)}) copy-start(f32[32,1,320]{2,1,0:T(1,128)S(1)} %broadcast_in_dim.2.cum_ref) | copy-start | bytes 122884
  71.3 1.9 collective-permute-start.10
  71.7 2.3 collective-permute-start.3
  73.4 9.4 %copy-start.5 = (f32[2,8,128,128]{3,2,1,0:T(8,128)}, f32[2,8,128,128]{3,2,1,0:T(8,128)S(1)}, u32[]{:S(2)}) copy-start(f32[2,8,128,128]{3,2,1,0:T(8,128)S(1)} %get-tuple-element.35) | copy-start | bytes 3145732
  73.6 9.2 %collective-permute-start.11 = (bf16[8,128,128]{2,1,0:T(8,128)(2,1)S(1)}, bf16[8,128,128]{2,1,0:T(8,128)(2,1)S(1)}, u32[]{:S(2)}, u32[]{:S(2)}) collective-permute-start(bf16[8,128,128]{2,1,0:T(8,128)(2,1)S(1)} %select_convert_fusion.4), channel_id=1, source_target_pairs={{0,2},{1,3},{2,0},{3,1},{4,6},{5,7},{6,4},{7,5},{8,10},{9,11},{10,... | collective-permute-start | bytes 786440 | tf_op jit(solution)/shard_map/ppermute | solution.py:337
  74.3 13.5 %collective-permute-start.4 = (bf16[8,128,128]{2,1,0:T(8,128)(2,1)S(1)}, bf16[8,128,128]{2,1,0:T(8,128)(2,1)S(1)}, u32[]{:S(2)}, u32[]{:S(2)}) collective-permute-start(bf16[8,128,128]{2,1,0:T(8,128)(2,1)S(1)} %select_convert_fusion.7), channel_id=1, source_target_pairs={{0,2},{1,3},{2,0},{3,1},{4,6},{5,7},{6,4},{7,5},{8,10},{9,11},{10,... | collective-permute-start | bytes 786440 | tf_op jit(solution)/shard_map/ppermute | solution.py:337
  83.1 9.0 %collective-permute-start.12 = (bf16[8,128,128]{2,1,0:T(8,128)(2,1)S(1)}, bf16[8,128,128]{2,1,0:T(8,128)(2,1)S(1)}, u32[]{:S(2)}, u32[]{:S(2)}) collective-permute-start(bf16[8,128,128]{2,1,0:T(8,128)(2,1)S(1)} %fusion.3), channel_id=1, source_target_pairs={{2,6},{3,7},{4,0},{5,1},{6,10},{7,11},{8,4},{9,5},{10,14},{11,15},... | collective-permute-start | bytes 786440 | tf_op jit(solution)/shard_map/ppermute | solution.py:344
  88.8 11.1 %collective-permute-start.5 = (bf16[8,128,128]{2,1,0:T(8,128)(2,1)S(1)}, bf16[8,128,128]{2,1,0:T(8,128)(2,1)S(1)}, u32[]{:S(2)}, u32[]{:S(2)}) collective-permute-start(bf16[8,128,128]{2,1,0:T(8,128)(2,1)S(1)} %fusion.1), channel_id=1, source_target_pairs={{2,6},{3,7},{4,0},{5,1},{6,10},{7,11},{8,4},{9,5},{10,14},{11,15},... | collective-permute-start | bytes 786440 | tf_op jit(solution)/shard_map/ppermute | solution.py:344
  92.1 7.9 %copy-start.20 = (bf16[8,128,128]{2,1,0:T(8,128)(2,1)}, bf16[8,128,128]{2,1,0:T(8,128)(2,1)S(1)}, u32[]{:S(2)}) copy-start(bf16[8,128,128]{2,1,0:T(8,128)(2,1)S(1)} %collective-permute-done.12) | copy-start | bytes 786436
  92.1 13.6 %collective-permute-start.13 = (bf16[8,128,128]{2,1,0:T(8,128)(2,1)S(1)}, bf16[8,128,128]{2,1,0:T(8,128)(2,1)}, u32[]{:S(2)}, u32[]{:S(2)}) collective-permute-start(bf16[8,128,128]{2,1,0:T(8,128)(2,1)S(1)} %collective-permute-done.12), channel_id=1, source_target_pairs={{2,6},{3,7},{4,0},{5,1},{6,10},{7,11},{8,4},{9,5},{10,14},{11,15},... | collective-permute-start | bytes 786440 | tf_op jit(solution)/shard_map/ppermute | solution.py:344
  99.9 17.2 %copy-start.19 = (bf16[8,128,128]{2,1,0:T(8,128)(2,1)}, bf16[8,128,128]{2,1,0:T(8,128)(2,1)S(1)}, u32[]{:S(2)}) copy-start(bf16[8,128,128]{2,1,0:T(8,128)(2,1)S(1)} %collective-permute-done.5) | copy-start | bytes 786436
  99.9 11.3 %collective-permute-start.6 = (bf16[8,128,128]{2,1,0:T(8,128)(2,1)S(1)}, bf16[8,128,128]{2,1,0:T(8,128)(2,1)}, u32[]{:S(2)}, u32[]{:S(2)}) collective-permute-start(bf16[8,128,128]{2,1,0:T(8,128)(2,1)S(1)} %collective-permute-done.5), channel_id=1, source_target_pairs={{2,6},{3,7},{4,0},{5,1},{6,10},{7,11},{8,4},{9,5},{10,14},{11,15},... | collective-permute-start | bytes 786440 | tf_op jit(solution)/shard_map/ppermute | solution.py:344
  105.7 11.4 %collective-permute-start.14 = (bf16[8,128,128]{2,1,0:T(8,128)(2,1)}, bf16[8,128,128]{2,1,0:T(8,128)(2,1)}, u32[]{:S(2)}, u32[]{:S(2)}) collective-permute-start(bf16[8,128,128]{2,1,0:T(8,128)(2,1)} %collective-permute-done.13), channel_id=1, source_target_pairs={{2,6},{3,7},{4,0},{5,1},{6,10},{7,11},{8,4},{9,5},{10,14},{11,15},... | collective-permute-start | bytes 786440 | tf_op jit(solution)/shard_map/ppermute | solution.py:344
  111.3 9.7 %collective-permute-start.7 = (bf16[8,128,128]{2,1,0:T(8,128)(2,1)}, bf16[8,128,128]{2,1,0:T(8,128)(2,1)}, u32[]{:S(2)}, u32[]{:S(2)}) collective-permute-start(bf16[8,128,128]{2,1,0:T(8,128)(2,1)} %collective-permute-done.6), channel_id=1, source_target_pairs={{2,6},{3,7},{4,0},{5,1},{6,10},{7,11},{8,4},{9,5},{10,14},{11,15},... | collective-permute-start | bytes 786440 | tf_op jit(solution)/shard_map/ppermute | solution.py:344
  118.5 7.2 %collective-permute-start.15 = (bf16[8,128,128]{2,1,0:T(8,128)(2,1)S(1)}, bf16[8,128,128]{2,1,0:T(8,128)(2,1)}, u32[]{:S(2)}, u32[]{:S(2)}) collective-permute-start(bf16[8,128,128]{2,1,0:T(8,128)(2,1)S(1)} %add_convert_fusion), channel_id=1, source_target_pairs={{0,2},{1,3},{2,0},{3,1},{4,6},{5,7},{6,4},{7,5},{8,10},{9,11},{10,... | collective-permute-start | bytes 786440 | tf_op jit(solution)/shard_map/ppermute | solution.py:349
  121.0 7.4 %copy-start.22 = (f32[8]{0:T(128)S(1)}, f32[8]{0:T(128)}, u32[]{:S(2)}) copy-start(f32[8]{0:T(128)} %get-tuple-element.52) | copy-start | bytes 100
  123.0 14.9 %collective-permute-start.8 = (bf16[8,128,128]{2,1,0:T(8,128)(2,1)}, bf16[8,128,128]{2,1,0:T(8,128)(2,1)}, u32[]{:S(2)}, u32[]{:S(2)}) collective-permute-start(bf16[8,128,128]{2,1,0:T(8,128)(2,1)} %add_convert_fusion.1), channel_id=1, source_target_pairs={{0,2},{1,3},{2,0},{3,1},{4,6},{5,7},{6,4},{7,5},{8,10},{9,11},{10,... | collective-permute-start | bytes 786440 | tf_op jit(solution)/shard_map/ppermute | solution.py:349
  128.3 11.8 %collective-permute-start.16 = (bf16[2,8,128,128]{3,2,1,0:T(8,128)(2,1)}, bf16[2,8,128,128]{3,2,1,0:T(8,128)(2,1)}, u32[]{:S(2)}, u32[]{:S(2)}) collective-permute-start(bf16[2,8,128,128]{3,2,1,0:T(8,128)(2,1)} %select_convert_fusion), channel_id=1, source_target_pairs={{0,1},{1,0},{2,3},{3,2},{4,5},{5,4},{6,7},{7,6},{8,9},{9,8},{10,11... | collective-permute-start | bytes 1572872 | tf_op jit(solution)/shard_map/ppermute | solution.py:359
  139.6 2.1 collective-permute-start.9
  (16 other events, 35.8 us)
